TPU v7x, 128 devices: a whole 4x4x4 slice. The times are simulated.
128 devices in a mesh: section: 8 (over x, core), kv: 16 (over y, z).
Axes of the slice: x: 4, y: 4, z: 4, core: 2. Of those that a mesh axis runs over, the one named last changes fastest.
Arguments:
- queries: bfloat16 [1024, 8192], P(('section', 'kv')), may hold values from -72 to 72
- new_keys: bfloat16 [1024, 1024], P(('section', 'kv')), may hold values from -6 to 6
- new_values: bfloat16 [1024, 1024], P(('section', 'kv')), may hold values from -6 to 6
- prefix_keys: bfloat16 [131072, 1024], P(('section', 'kv')), may hold values from -20 to 20
- prefix_values: bfloat16 [131072, 1024], P(('section', 'kv')), may hold values from -6 to 6
- lengths: int32 [8], replicated, may hold values from 1024 to 16384, as said below
Outputs:
- attended: bfloat16 [1024, 8192], P(('section', 'kv'))
Inputs may be any that keep to these rules, and one draw needn't show every extreme that they name: `lengths`: some section has 16384 live rows and another 16384 // 16.
All inputs are finite; a program needn't handle non-finite values.
Results may differ from a plain program's by a relative error of at most 0.005.
Values may be sent and summed in bfloat16 or wider, within the bound.
No kernel may reach another device: no remote copies, remote signals or barrier semaphores. Data moves between devices by JAX's collectives and lax.ppermute only.
A program may use at most 256 MiB of HBM per device.

v0:
```python
import math

import jax
import jax.numpy as jnp
from jax import lax
from jax.sharding import PartitionSpec as P

H = 64
KVH = 8
DH = 128


NEG = -1e30


def joined(value, axis, join):
    pieces = jax.tree.map(lambda part: lax.all_gather(part, axis), value)
    head = jax.tree.map(lambda part: part[0], pieces)
    tail = jax.tree.map(lambda part: part[1:], pieces)
    subtotal, _ = lax.scan(lambda subtotal, slab: (join(subtotal, slab), None), head, tail)
    return subtotal


def shifted(value, axis, steps):
    count = lax.axis_size(axis)
    pairs = [(source, (source + steps) % count) for source in range(count)]
    return lax.ppermute(value, axis, pairs)


def fold_block(state, grouped_query_rows, cached_key_block, cached_value_block, allowed):
    weighted, peaks, totals = state
    scores = jnp.einsum(
        "cwhv,owv->whco", grouped_query_rows, cached_key_block, preferred_element_type=jnp.float32
    ) * grouped_query_rows.shape[-1] ** (-0.5)
    scores = jnp.where(allowed, scores, NEG)
    raised = jnp.maximum(peaks, jnp.max(scores, axis=-1))
    weights = jnp.exp(scores - raised[..., None])
    factor = jnp.exp(peaks - raised)
    totals = totals * factor + jnp.sum(weights, axis=-1)
    weighted = weighted * factor[..., None] + jnp.einsum(
        "cjzm,mcv->cjzv",
        weights.astype(jnp.bfloat16),
        cached_value_block,
        preferred_element_type=jnp.float32,
    )
    return (weighted, raised, totals)


def empty_state(kv_heads, group_size, count, head_dim):
    return (
        jnp.zeros((kv_heads, group_size, count, head_dim), jnp.float32),
        jnp.full((kv_heads, group_size, count), NEG, jnp.float32),
        jnp.zeros((kv_heads, group_size, count), jnp.float32),
    )


def join_pair(left, right):
    raised = jnp.maximum(left[1], right[1])
    left_scale = jnp.exp(left[1] - raised)
    right_scale = jnp.exp(right[1] - raised)
    return (
        left[0] * left_scale[..., None] + right[0] * right_scale[..., None],
        raised,
        left[2] * left_scale + right[2] * right_scale,
    )


def sweep(state, grouped_query_rows, key_rows, value_rows, offset, limit, stop, block_rows):
    kv_heads = grouped_query_rows.shape[1]
    head_dim = grouped_query_rows.shape[3]

    def visit_block(turn, carried):
        start = turn * block_rows
        cached_key_block = lax.dynamic_slice_in_dim(key_rows, start, block_rows, 0).reshape(
            block_rows, kv_heads, head_dim
        )
        cached_value_block = lax.dynamic_slice_in_dim(value_rows, start, block_rows, 0).reshape(
            block_rows, kv_heads, head_dim
        )
        places = offset + start + jnp.arange(block_rows, dtype=jnp.int32)
        allowed = (places < limit)[None, :]
        active = jnp.logical_and(offset + start < limit, turn < stop)
        return lax.cond(
            active,
            lambda inner: fold_block(
                inner, grouped_query_rows, cached_key_block, cached_value_block, allowed
            ),
            lambda inner: inner,
            carried,
        )

    return lax.fori_loop(0, key_rows.shape[0] // block_rows, visit_block, state)


def on_device(queries, new_keys, new_values, prefix_keys, prefix_values, lengths):
    q_dev = queries.shape[0]
    kv_dev = prefix_keys.shape[0]
    group_size = H // KVH
    section_id = lax.axis_index("section")
    kv_slot = lax.axis_index("kv")
    length_here = lengths[section_id]
    complete_query_rows, whole_keys, whole_values = (
        lax.all_gather(queries, "kv", axis=0, tiled=True),
        lax.all_gather(new_keys, "kv", axis=0, tiled=True),
        lax.all_gather(new_values, "kv", axis=0, tiled=True),
    )
    query_row_count = complete_query_rows.shape[0]
    grouped_query_rows = complete_query_rows.reshape(query_row_count, KVH, group_size, DH)
    half_rows = kv_dev // 2
    block_rows = math.gcd(half_rows, 256)
    offset = kv_slot * kv_dev
    state = empty_state(KVH, group_size, query_row_count, DH)
    state = sweep(
        state,
        grouped_query_rows,
        prefix_keys,
        prefix_values,
        offset,
        length_here,
        kv_dev // block_rows,
        block_rows,
    )
    merged = joined((state[0], state[1], state[2]), "kv", join_pair)
    first_row = kv_slot * q_dev
    mine = (
        lax.dynamic_slice_in_dim(merged[0], first_row, q_dev, 2),
        lax.dynamic_slice_in_dim(merged[1], first_row, q_dev, 2),
        lax.dynamic_slice_in_dim(merged[2], first_row, q_dev, 2),
    )
    local_grouped_queries = queries.reshape(q_dev, KVH, group_size, DH)
    own_allowed = (
        jnp.arange(query_row_count, dtype=jnp.int32)[None, :]
        <= (kv_slot * q_dev + jnp.arange(q_dev, dtype=jnp.int32))[:, None]
    )
    own_state = fold_block(
        empty_state(KVH, group_size, q_dev, DH),
        local_grouped_queries,
        whole_keys.reshape(query_row_count, KVH, DH),
        whole_values.reshape(query_row_count, KVH, DH),
        own_allowed,
    )
    weighted, peaks, totals = join_pair(mine, own_state)
    result = weighted / totals[..., None]
    result = jnp.transpose(result, (2, 0, 1, 3)).reshape(q_dev, H * DH).astype(jnp.bfloat16)
    return shifted(result, "section", 1)


def solution(mesh):
    return jax.shard_map(
        on_device,
        mesh=mesh,
        in_specs=(
            P(("section", "kv"), None),
            P(("section", "kv"), None),
            P(("section", "kv"), None),
            P(("section", "kv"), None),
            P(("section", "kv"), None),
            P(),
        ),
        out_specs=P(("section", "kv"), None),
        check_vma=False,
    )
```

profile of v0, /device:TPU:0, one launch (start us, length us, event | category | flops | bytes accessed | tf_op | source)
XLA Modules:
  0.0 656.3 jit_solution(16355326951220129403)
XLA Ops:
  7.3 3.9 copy.29
  11.3 2.5 copy.31
  14.5 42.8 %all-gather.6.cloned.1.call-done = bf16[128,8192]{1,0:T(8,128)(2,1)} async-done(((bf16[8,8192]{1,0:T(8,128)(2,1)}), bf16[128,8192]{1,0:T(8,128)(2,1)}) %all-gather.6.cloned.1.call-update) | async-done | bytes 2097168 | tf_op jit(solution)/shard_map/all_gather | solution.py:103
  57.3 4.1 copy.28
  61.4 3.0 copy.30
  64.5 2.5 broadcast_in_dim.56
  67.0 52.2 %while.31 = (s32[]{:T(128)}, f32[8,8,128,128]{3,2,1,0:T(8,128)}, f32[8,8,128]{2,1,0:T(8,128)S(1)}, f32[8,8,128]{2,1,0:T(8,128)S(1)}, s32[]{:T(128)}, /*index=5*/...) while((s32[]{:T(128)}, f32[8,8,128,128]{3,2,1,0:T(8,128)}, ...), condition=%wide.region_5.6_spmd, body=%wide.region_0.5_spmd.sunk | while | flops 1098924544 | bytes 72879488 | solution.py:92
  67.7 12.4 %conditional.2 = ((f32[8,8,128,128]{3,2,1,0:T(8,128)}, f32[8,8,128]{2,1,0:T(8,128)S(1)}, f32[8,8,128]{2,1,0:T(8,128)S(1)})) conditional(s32[]{:T(128)} %convert_element_type.36, (f32[8,8,128,128]{3,2,1,0:T(8,128)}, f32[8,8,128]{2,1,0:T(8,128)S(1)}, f32[8,8,128]{2,1,0:T(8,128)S(1)}) %tuple.72, (s32[]{:T(128)}, s32[1,256]{1,0:T(1,128)S(1)}, s32[]{:T(128)}, ...), branch_computations={%region_1.0_spmd, %region_2.4_spmd} | conditional | flops 1098924544 | bytes 72878216 | solution.py:83
  69.7 2.1 bitcast_reduce_fusion
  71.8 2.3 fusion.4
  74.1 3.9 multiply_add_fusion
  78.0 2.0 copy-done.1
  80.7 12.4 %conditional.2 = ((f32[8,8,128,128]{3,2,1,0:T(8,128)}, f32[8,8,128]{2,1,0:T(8,128)S(1)}, f32[8,8,128]{2,1,0:T(8,128)S(1)})) conditional(s32[]{:T(128)} %convert_element_type.36, (f32[8,8,128,128]{3,2,1,0:T(8,128)}, f32[8,8,128]{2,1,0:T(8,128)S(1)}, f32[8,8,128]{2,1,0:T(8,128)S(1)}) %tuple.72, (s32[]{:T(128)}, s32[1,256]{1,0:T(1,128)S(1)}, s32[]{:T(128)}, ...), branch_computations={%region_1.0_spmd, %region_2.4_spmd} | conditional | flops 1098924544 | bytes 72878216 | solution.py:83
  82.8 2.1 bitcast_reduce_fusion
  84.8 2.3 fusion.4
  87.2 3.9 multiply_add_fusion
  93.8 12.4 %conditional.2 = ((f32[8,8,128,128]{3,2,1,0:T(8,128)}, f32[8,8,128]{2,1,0:T(8,128)S(1)}, f32[8,8,128]{2,1,0:T(8,128)S(1)})) conditional(s32[]{:T(128)} %convert_element_type.36, (f32[8,8,128,128]{3,2,1,0:T(8,128)}, f32[8,8,128]{2,1,0:T(8,128)S(1)}, f32[8,8,128]{2,1,0:T(8,128)S(1)}) %tuple.72, (s32[]{:T(128)}, s32[1,256]{1,0:T(1,128)S(1)}, s32[]{:T(128)}, ...), branch_computations={%region_1.0_spmd, %region_2.4_spmd} | conditional | flops 1098924544 | bytes 72878216 | solution.py:83
  95.8 2.1 bitcast_reduce_fusion
  97.9 2.3 fusion.4
  100.2 3.9 multiply_add_fusion
  106.8 12.3 %conditional.2 = ((f32[8,8,128,128]{3,2,1,0:T(8,128)}, f32[8,8,128]{2,1,0:T(8,128)S(1)}, f32[8,8,128]{2,1,0:T(8,128)S(1)})) conditional(s32[]{:T(128)} %convert_element_type.36, (f32[8,8,128,128]{3,2,1,0:T(8,128)}, f32[8,8,128]{2,1,0:T(8,128)S(1)}, f32[8,8,128]{2,1,0:T(8,128)S(1)}) %tuple.72, (s32[]{:T(128)}, s32[1,256]{1,0:T(1,128)S(1)}, s32[]{:T(128)}, ...), branch_computations={%region_1.0_spmd, %region_2.4_spmd} | conditional | flops 1098924544 | bytes 72878216 | solution.py:83
  108.9 2.0 bitcast_reduce_fusion
  110.9 2.3 fusion.4
  113.3 3.9 multiply_add_fusion
  119.9 23.4 %all_gather.34 = bf16[128,1024]{1,0:T(8,128)(2,1)S(1)} all-gather(bf16[8,1024]{1,0:T(8,128)(2,1)S(1)} %copy-done.4), channel_id=1, replica_groups=mesh['section'=8,'kv'=16] {'kv'}, dimensions={0}, use_global_device_ids=true | all-gather | bytes 278528 | tf_op jit(solution)/shard_map/all_gather | solution.py:104
  143.5 22.1 %all_gather.35 = bf16[128,1024]{1,0:T(8,128)(2,1)S(1)} all-gather(bf16[8,1024]{1,0:T(8,128)(2,1)S(1)} %copy-done.5), channel_id=1, replica_groups=mesh['section'=8,'kv'=16] {'kv'}, dimensions={0}, use_global_device_ids=true | all-gather | bytes 278528 | tf_op jit(solution)/shard_map/all_gather | solution.py:105
  166.4 24.4 %all-gather.1 = f32[128,8,128]{2,1,0:T(8,128)S(1)} all-gather(f32[8,8,128]{2,1,0:T(8,128)S(1)} %get-tuple-element.332), channel_id=3, replica_groups=mesh['section'=8,'kv'=16] {'kv'}, dimensions={0}, use_global_device_ids=true | all-gather | bytes 557056 | tf_op jit(solution)/shard_map/all_gather | solution.py:17
  190.9 23.0 %all-gather.2 = f32[128,8,128]{2,1,0:T(8,128)S(1)} all-gather(f32[8,8,128]{2,1,0:T(8,128)S(1)} %get-tuple-element.333), channel_id=4, replica_groups=mesh['section'=8,'kv'=16] {'kv'}, dimensions={0}, use_global_device_ids=true | all-gather | bytes 557056 | tf_op jit(solution)/shard_map/all_gather | solution.py:17
  214.0 280.1 %all-gather.8.cloned.1.call-done = f32[128,8,128,128]{3,2,1,0:T(8,128)} async-done(((f32[8,8,128,128]{3,2,1,0:T(8,128)}), f32[128,8,128,128]{3,2,1,0:T(8,128)}) %all-gather.8.cloned.1.call-update) | async-done | bytes 67108880 | tf_op jit(solution)/shard_map/all_gather | solution.py:17
  494.1 40.7 %slice.34 = f32[120,8,128,128]{3,2,1,0:T(8,128)} slice(f32[128,8,128,128]{3,2,1,0:T(8,128)} %all-gather.8.cloned.1.call-done), slice={[8:128], [0:8], [0:128], [0:128]} | slice | bytes 125829120 | tf_op jit(solution)/shard_map/slice | solution.py:19
  534.8 4.6 slice.30
  539.4 101.7 %while.32 = (s32[]{:T(128)}, f32[8,8,128,128]{3,2,1,0:T(8,128)}, f32[8,8,128]{2,1,0:T(8,128)S(1)}, f32[8,8,128]{2,1,0:T(8,128)S(1)}, f32[15,8,8,128]{3,2,1,0:T(8...) while((s32[]{:T(128)}, f32[8,8,128,128]{3,2,1,0:T(8,128)}, ...), condition=%wide.region_7.8_spmd, body=%wide.region_6.7_spmd.sunk | while | flops 3194882 | bytes 12910685 | solution.py:20
  539.5 6.8 %fusion.40 = f32[8,8,128,128]{3,2,1,0:T(8,128)} fusion(f32[15,8,8,128,128]{4,3,2,1,0:T(8,128)} %get-tuple-element.577, s32[]{:T(128)} %get-tuple-element.564, f32[8,8,128,128]{3,2,1,0:T(8,128)} %get-tuple-element.565, f32[8,8,128]{2,1,0:T(8,128)S(1)} %get-tuple-element.513, f32[8,8,128]{2,1,0:T(8,128)S(1)} %get-tuple-element.514), kind=kLoop, calls=%fused_computation.1.clone.1 | loop fusion | flops 3145728 | bytes 12648452 | tf_op jit(solution)/shard_map/while/body/eval_jaxpr/add | solution.py:62
  546.2 6.8 %fusion.40 = f32[8,8,128,128]{3,2,1,0:T(8,128)} fusion(f32[15,8,8,128,128]{4,3,2,1,0:T(8,128)} %get-tuple-element.577, s32[]{:T(128)} %get-tuple-element.564, f32[8,8,128,128]{3,2,1,0:T(8,128)} %get-tuple-element.565, f32[8,8,128]{2,1,0:T(8,128)S(1)} %get-tuple-element.513, f32[8,8,128]{2,1,0:T(8,128)S(1)} %get-tuple-element.514), kind=kLoop, calls=%fused_computation.1.clone.1 | loop fusion | flops 3145728 | bytes 12648452 | tf_op jit(solution)/shard_map/while/body/eval_jaxpr/add | solution.py:62
  553.0 6.8 %fusion.40 = f32[8,8,128,128]{3,2,1,0:T(8,128)} fusion(f32[15,8,8,128,128]{4,3,2,1,0:T(8,128)} %get-tuple-element.577, s32[]{:T(128)} %get-tuple-element.564, f32[8,8,128,128]{3,2,1,0:T(8,128)} %get-tuple-element.565, f32[8,8,128]{2,1,0:T(8,128)S(1)} %get-tuple-element.513, f32[8,8,128]{2,1,0:T(8,128)S(1)} %get-tuple-element.514), kind=kLoop, calls=%fused_computation.1.clone.1 | loop fusion | flops 3145728 | bytes 12648452 | tf_op jit(solution)/shard_map/while/body/eval_jaxpr/add | solution.py:62
  559.8 6.8 %fusion.40 = f32[8,8,128,128]{3,2,1,0:T(8,128)} fusion(f32[15,8,8,128,128]{4,3,2,1,0:T(8,128)} %get-tuple-element.577, s32[]{:T(128)} %get-tuple-element.564, f32[8,8,128,128]{3,2,1,0:T(8,128)} %get-tuple-element.565, f32[8,8,128]{2,1,0:T(8,128)S(1)} %get-tuple-element.513, f32[8,8,128]{2,1,0:T(8,128)S(1)} %get-tuple-element.514), kind=kLoop, calls=%fused_computation.1.clone.1 | loop fusion | flops 3145728 | bytes 12648452 | tf_op jit(solution)/shard_map/while/body/eval_jaxpr/add | solution.py:62
  566.6 6.8 %fusion.40 = f32[8,8,128,128]{3,2,1,0:T(8,128)} fusion(f32[15,8,8,128,128]{4,3,2,1,0:T(8,128)} %get-tuple-element.577, s32[]{:T(128)} %get-tuple-element.564, f32[8,8,128,128]{3,2,1,0:T(8,128)} %get-tuple-element.565, f32[8,8,128]{2,1,0:T(8,128)S(1)} %get-tuple-element.513, f32[8,8,128]{2,1,0:T(8,128)S(1)} %get-tuple-element.514), kind=kLoop, calls=%fused_computation.1.clone.1 | loop fusion | flops 3145728 | bytes 12648452 | tf_op jit(solution)/shard_map/while/body/eval_jaxpr/add | solution.py:62
  573.4 6.8 %fusion.40 = f32[8,8,128,128]{3,2,1,0:T(8,128)} fusion(f32[15,8,8,128,128]{4,3,2,1,0:T(8,128)} %get-tuple-element.577, s32[]{:T(128)} %get-tuple-element.564, f32[8,8,128,128]{3,2,1,0:T(8,128)} %get-tuple-element.565, f32[8,8,128]{2,1,0:T(8,128)S(1)} %get-tuple-element.513, f32[8,8,128]{2,1,0:T(8,128)S(1)} %get-tuple-element.514), kind=kLoop, calls=%fused_computation.1.clone.1 | loop fusion | flops 3145728 | bytes 12648452 | tf_op jit(solution)/shard_map/while/body/eval_jaxpr/add | solution.py:62
  580.1 6.8 %fusion.40 = f32[8,8,128,128]{3,2,1,0:T(8,128)} fusion(f32[15,8,8,128,128]{4,3,2,1,0:T(8,128)} %get-tuple-element.577, s32[]{:T(128)} %get-tuple-element.564, f32[8,8,128,128]{3,2,1,0:T(8,128)} %get-tuple-element.565, f32[8,8,128]{2,1,0:T(8,128)S(1)} %get-tuple-element.513, f32[8,8,128]{2,1,0:T(8,128)S(1)} %get-tuple-element.514), kind=kLoop, calls=%fused_computation.1.clone.1 | loop fusion | flops 3145728 | bytes 12648452 | tf_op jit(solution)/shard_map/while/body/eval_jaxpr/add | solution.py:62
  586.9 6.8 %fusion.40 = f32[8,8,128,128]{3,2,1,0:T(8,128)} fusion(f32[15,8,8,128,128]{4,3,2,1,0:T(8,128)} %get-tuple-element.577, s32[]{:T(128)} %get-tuple-element.564, f32[8,8,128,128]{3,2,1,0:T(8,128)} %get-tuple-element.565, f32[8,8,128]{2,1,0:T(8,128)S(1)} %get-tuple-element.513, f32[8,8,128]{2,1,0:T(8,128)S(1)} %get-tuple-element.514), kind=kLoop, calls=%fused_computation.1.clone.1 | loop fusion | flops 3145728 | bytes 12648452 | tf_op jit(solution)/shard_map/while/body/eval_jaxpr/add | solution.py:62
  593.7 6.8 %fusion.40 = f32[8,8,128,128]{3,2,1,0:T(8,128)} fusion(f32[15,8,8,128,128]{4,3,2,1,0:T(8,128)} %get-tuple-element.577, s32[]{:T(128)} %get-tuple-element.564, f32[8,8,128,128]{3,2,1,0:T(8,128)} %get-tuple-element.565, f32[8,8,128]{2,1,0:T(8,128)S(1)} %get-tuple-element.513, f32[8,8,128]{2,1,0:T(8,128)S(1)} %get-tuple-element.514), kind=kLoop, calls=%fused_computation.1.clone.1 | loop fusion | flops 3145728 | bytes 12648452 | tf_op jit(solution)/shard_map/while/body/eval_jaxpr/add | solution.py:62
  600.5 6.8 %fusion.40 = f32[8,8,128,128]{3,2,1,0:T(8,128)} fusion(f32[15,8,8,128,128]{4,3,2,1,0:T(8,128)} %get-tuple-element.577, s32[]{:T(128)} %get-tuple-element.564, f32[8,8,128,128]{3,2,1,0:T(8,128)} %get-tuple-element.565, f32[8,8,128]{2,1,0:T(8,128)S(1)} %get-tuple-element.513, f32[8,8,128]{2,1,0:T(8,128)S(1)} %get-tuple-element.514), kind=kLoop, calls=%fused_computation.1.clone.1 | loop fusion | flops 3145728 | bytes 12648452 | tf_op jit(solution)/shard_map/while/body/eval_jaxpr/add | solution.py:62
  607.3 6.8 %fusion.40 = f32[8,8,128,128]{3,2,1,0:T(8,128)} fusion(f32[15,8,8,128,128]{4,3,2,1,0:T(8,128)} %get-tuple-element.577, s32[]{:T(128)} %get-tuple-element.564, f32[8,8,128,128]{3,2,1,0:T(8,128)} %get-tuple-element.565, f32[8,8,128]{2,1,0:T(8,128)S(1)} %get-tuple-element.513, f32[8,8,128]{2,1,0:T(8,128)S(1)} %get-tuple-element.514), kind=kLoop, calls=%fused_computation.1.clone.1 | loop fusion | flops 3145728 | bytes 12648452 | tf_op jit(solution)/shard_map/while/body/eval_jaxpr/add | solution.py:62
  614.1 6.8 %fusion.40 = f32[8,8,128,128]{3,2,1,0:T(8,128)} fusion(f32[15,8,8,128,128]{4,3,2,1,0:T(8,128)} %get-tuple-element.577, s32[]{:T(128)} %get-tuple-element.564, f32[8,8,128,128]{3,2,1,0:T(8,128)} %get-tuple-element.565, f32[8,8,128]{2,1,0:T(8,128)S(1)} %get-tuple-element.513, f32[8,8,128]{2,1,0:T(8,128)S(1)} %get-tuple-element.514), kind=kLoop, calls=%fused_computation.1.clone.1 | loop fusion | flops 3145728 | bytes 12648452 | tf_op jit(solution)/shard_map/while/body/eval_jaxpr/add | solution.py:62
  620.8 6.8 %fusion.40 = f32[8,8,128,128]{3,2,1,0:T(8,128)} fusion(f32[15,8,8,128,128]{4,3,2,1,0:T(8,128)} %get-tuple-element.577, s32[]{:T(128)} %get-tuple-element.564, f32[8,8,128,128]{3,2,1,0:T(8,128)} %get-tuple-element.565, f32[8,8,128]{2,1,0:T(8,128)S(1)} %get-tuple-element.513, f32[8,8,128]{2,1,0:T(8,128)S(1)} %get-tuple-element.514), kind=kLoop, calls=%fused_computation.1.clone.1 | loop fusion | flops 3145728 | bytes 12648452 | tf_op jit(solution)/shard_map/while/body/eval_jaxpr/add | solution.py:62
  627.6 6.8 %fusion.40 = f32[8,8,128,128]{3,2,1,0:T(8,128)} fusion(f32[15,8,8,128,128]{4,3,2,1,0:T(8,128)} %get-tuple-element.577, s32[]{:T(128)} %get-tuple-element.564, f32[8,8,128,128]{3,2,1,0:T(8,128)} %get-tuple-element.565, f32[8,8,128]{2,1,0:T(8,128)S(1)} %get-tuple-element.513, f32[8,8,128]{2,1,0:T(8,128)S(1)} %get-tuple-element.514), kind=kLoop, calls=%fused_computation.1.clone.1 | loop fusion | flops 3145728 | bytes 12648452 | tf_op jit(solution)/shard_map/while/body/eval_jaxpr/add | solution.py:62
  634.4 6.8 %fusion.40 = f32[8,8,128,128]{3,2,1,0:T(8,128)} fusion(f32[15,8,8,128,128]{4,3,2,1,0:T(8,128)} %get-tuple-element.577, s32[]{:T(128)} %get-tuple-element.564, f32[8,8,128,128]{3,2,1,0:T(8,128)} %get-tuple-element.565, f32[8,8,128]{2,1,0:T(8,128)S(1)} %get-tuple-element.513, f32[8,8,128]{2,1,0:T(8,128)S(1)} %get-tuple-element.514), kind=kLoop, calls=%fused_computation.1.clone.1 | loop fusion | flops 3145728 | bytes 12648452 | tf_op jit(solution)/shard_map/while/body/eval_jaxpr/add | solution.py:62
  643.2 5.6 collective-permute-done
  (92 shorter events, 20.4 us)
Async XLA Ops:
  6.5 4.7 copy-start.2
  6.5 50.8 %all-gather.6.cloned.1.call-start = ((), (), s32[]{:S(2)}) async-start(), calls=%async_computation | async-start | bytes 2228224 | tf_op jit(solution)/shard_map/all_gather | solution.py:103
  7.3 486.9 %all-gather.8.cloned.1.call-start = ((), (), s32[]{:S(2)}) async-start(), calls=%async_computation.1 | async-start | bytes 71303168 | tf_op jit(solution)/shard_map/all_gather | solution.py:17
  7.3 6.5 copy-start.6
  71.8 2.3 copy-start
  78.0 2.0 copy-start.1
  84.8 2.3 copy-start
  91.1 2.0 copy-start.1
  97.9 2.3 copy-start
  104.1 2.0 copy-start.1
  110.9 2.3 copy-start
  117.2 2.0 copy-start.1
  119.2 0.7 copy-start.4
  119.2 24.3 %copy-start.5 = (bf16[8,1024]{1,0:T(8,128)(2,1)S(1)}, bf16[8,1024]{1,0:T(8,128)(2,1)}, u32[]{:S(2)}) copy-start(bf16[8,1024]{1,0:T(8,128)(2,1)} %param.14) | copy-start | bytes 49156
  119.2 46.7 %copy-start.3 = (bf16[8,8192]{1,0:T(8,128)(2,1)S(1)}, bf16[8,8192]{1,0:T(8,128)(2,1)}, u32[]{:S(2)}) copy-start(bf16[8,8192]{1,0:T(8,128)(2,1)} %param.12) | copy-start | bytes 393220
  643.2 5.6 collective-permute-start
Sparse Core Ops, SparseCore 0:
  9.5 47.7 all-gather.5
  119.3 374.7 all-gather.7
where the time goes:
time: 658 us; the launch traced here: 656 us
  waiting for transfers between devices  329 us (50%)
  other arithmetic  114 us (17%)
  blocking collectives  93 us (14%)
  local copies, waits for them, and re-layouts  77.7 us (12%)
  matrix products  25.5 us (4%)
  between operations  13.6 us (2%)
    all_gather x1, waiting for transfers between devices, joined(): pieces = jax.tree.map(lambda part: lax.all_gather(part, axis), value)  280 us
    add x15, other arithmetic, join_pair(): left[0] * left_scale[..., None] + right[0] * right_scale[..., None]  101 us
    all_gather x2, blocking collectives, joined(): pieces = jax.tree.map(lambda part: lax.all_gather(part, axis), value)  47.5 us
    all_gather x1, waiting for transfers between devices, on_device(): lax.all_gather(queries, 'kv', axis=0, tiled=True)  42.8 us
    slice x3, local copies, waits for them, and re-layouts, joined(): tail = jax.tree.map(lambda part: part[1:], pieces)  40.8 us
    all_gather x1, blocking collectives, on_device(): lax.all_gather(new_keys, 'kv', axis=0, tiled=True)  23.4 us
    all_gather x1, blocking collectives, on_device(): lax.all_gather(new_values, 'kv', axis=0, tiled=True)  22.1 us
    dot_general x5, matrix products, fold_block(): jnp.einsum('cjzm,mcv->cjzv', weights.astype(jnp.bfloat16), cached_value_b...  17 us
  transfers between devices with their start and end apart: 3, of which 3 were waited for; matrix products, arithmetic and copies ran while one was open for 1% of the time, Pallas kernels for 0%

commit v1 on v0

v1 whole, which is shorter than its diff:
```python
import functools

import jax
import jax.numpy as jnp
from jax import lax
from jax.experimental import pallas as pl
from jax.experimental.pallas import tpu as pltpu
from jax.sharding import PartitionSpec as P

H = 64
KVH = 8
DH = 128
GROUP = H // KVH
WIDE = GROUP * DH

NEG = -1e30
FLOOR = -1e29
TINY = 1e-37
LOG2E = 1.4426950408889634
CHUNKS = 2


def attend(heads, lengths_ref, q_ref, k_ref, v_ref, nk_ref, nv_ref, o_ref, stats_ref):
    rows = q_ref.shape[0]
    keys = k_ref.shape[0]
    fresh = nk_ref.shape[0]
    step = pl.program_id(0)
    slot = lax.axis_index("kv")
    live = lengths_ref[lax.axis_index("section")] - slot * keys
    scale = DH**-0.5 * LOG2E

    @pl.when(step == 0)
    def _():
        stats_ref[...] = jnp.full(stats_ref.shape, FLOOR, jnp.float32)

    lanes = lax.broadcasted_iota(jnp.int32, (rows, DH), 1)
    own = jnp.logical_and(lanes < fresh, lanes + slot * fresh <= lax.broadcasted_iota(jnp.int32, (rows, DH), 0))
    stats_lane = lax.rem(lanes, 4 * 8)

    def padded(ref):
        blank = jnp.zeros((DH - fresh, DH), jnp.float32)
        return jnp.concatenate([ref[...].astype(jnp.float32), blank], axis=0).astype(jnp.bfloat16)

    new_k, new_v = padded(nk_ref), padded(nv_ref)
    ones = jnp.ones((DH, DH), jnp.bfloat16)
    new_v = jnp.concatenate([new_v, ones], axis=1)

    def contract(left, right, dim):
        return lax.dot_general(left, right, (((1,), (dim,)), ((), ())), preferred_element_type=jnp.float32)

    def finish(g, acc, peak):
        total = jnp.maximum(acc[:, DH:], TINY)
        o_ref[:, pl.ds(pl.multiple_of(step * WIDE + g * DH, DH), DH)] = (acc[:, :DH] / total).astype(jnp.bfloat16)
        stats_ref[...] = jnp.where(stats_lane == step * GROUP + g, peak + jnp.log2(total), stats_ref[...])

    def sweep(masked):
        k = k_ref[...]
        v = jnp.concatenate([v_ref[...], jnp.ones((keys, DH), jnp.bfloat16)], axis=1)
        allowed = lax.broadcasted_iota(jnp.int32, (1, keys), 1) < live
        for g in range(GROUP):
            q = q_ref[:, g * DH : (g + 1) * DH]
            s = contract(q, k, 1)
            if masked:
                s = jnp.where(allowed, s, NEG)
            t = jnp.where(own, contract(q, new_k, 1), NEG)
            peak = jnp.maximum(jnp.max(s, axis=1, keepdims=True), jnp.max(t, axis=1, keepdims=True))
            peak = jnp.maximum(peak * scale, FLOOR)
            w = jnp.exp2(s * scale - peak).astype(jnp.bfloat16)
            u = jnp.exp2(t * scale - peak).astype(jnp.bfloat16)
            finish(g, contract(w, v, 0) + contract(u, new_v, 0), peak)

    @pl.when(live >= keys)
    def _():
        sweep(False)

    @pl.when(jnp.logical_and(live > 0, live < keys))
    def _():
        sweep(True)

    @pl.when(live <= 0)
    def _():
        for g in range(GROUP):
            q = q_ref[:, g * DH : (g + 1) * DH]
            t = jnp.where(own, contract(q, new_k, 1), NEG)
            peak = jnp.maximum(jnp.max(t, axis=1, keepdims=True) * scale, FLOOR)
            u = jnp.exp2(t * scale - peak).astype(jnp.bfloat16)
            finish(g, contract(u, new_v, 0), peak)

    @pl.when(step == heads - 1)
    def _():
        whole = stats_ref[...]
        first = whole.astype(jnp.bfloat16)
        rest = whole - first.astype(jnp.float32)
        second = rest.astype(jnp.bfloat16)
        third = rest - second.astype(jnp.float32)
        picked = jnp.where(lanes < 32, first.astype(jnp.float32), jnp.where(lanes < 64, second.astype(jnp.float32), third))
        o_ref[:, heads * WIDE :] = picked.astype(jnp.bfloat16)


def attend_call(first, heads, lengths, q, keys, values, new_keys, new_values):
    rows, depth, fresh = q.shape[0], keys.shape[0], new_keys.shape[0]
    return pl.pallas_call(
        functools.partial(attend, heads),
        grid=(heads,),
        in_specs=[
            pl.BlockSpec(memory_space=pltpu.SMEM),
            pl.BlockSpec((rows, WIDE), lambda i: (0, i)),
            pl.BlockSpec((depth, DH), lambda i: (0, first + i)),
            pl.BlockSpec((depth, DH), lambda i: (0, first + i)),
            pl.BlockSpec((fresh, DH), lambda i: (0, first + i)),
            pl.BlockSpec((fresh, DH), lambda i: (0, first + i)),
        ],
        out_specs=pl.BlockSpec((rows, heads * WIDE + DH), lambda i: (0, 0)),
        out_shape=jax.ShapeDtypeStruct((rows, heads * WIDE + DH), jnp.bfloat16),
        scratch_shapes=[pltpu.VMEM((rows, DH), jnp.float32)],
        compiler_params=pltpu.CompilerParams(vmem_limit_bytes=32 * 1024 * 1024),
        name="attend",
    )(lengths, q, keys, values, new_keys, new_values)


def merge(heads, parts, x_ref, o_ref):
    rows = o_ref.shape[0]
    packed = x_ref[:, heads * WIDE :].astype(jnp.float32).reshape(parts, rows, DH)
    whole = packed[:, :, 0:32] + packed[:, :, 32:64] + packed[:, :, 64:96]
    peak = jnp.max(whole, axis=0, keepdims=True)
    w = jnp.exp2(whole - peak)
    w = w / jnp.sum(w, axis=0, keepdims=True)
    for h in range(heads * GROUP):
        x = x_ref[:, h * DH : (h + 1) * DH].astype(jnp.float32).reshape(parts, rows, DH)
        o_ref[:, h * DH : (h + 1) * DH] = jnp.sum(x * w[:, :, h : h + 1], axis=0).astype(jnp.bfloat16)


def merge_call(heads, parts, x):
    rows = x.shape[0] // parts
    return pl.pallas_call(
        functools.partial(merge, heads, parts),
        in_specs=[pl.BlockSpec(memory_space=pltpu.VMEM)],
        out_specs=pl.BlockSpec(memory_space=pltpu.VMEM),
        out_shape=jax.ShapeDtypeStruct((rows, heads * WIDE), jnp.bfloat16),
        compiler_params=pltpu.CompilerParams(vmem_limit_bytes=32 * 1024 * 1024),
        name="merge",
    )(x)


def on_device(queries, new_keys, new_values, prefix_keys, prefix_values, lengths):
    parts = lax.axis_size("kv")
    sections = lax.axis_size("section")
    rows = queries.shape[0]
    heads = KVH // CHUNKS
    results = []
    gathered = []
    for c in range(CHUNKS):
        own = queries[:, c * heads * WIDE : (c + 1) * heads * WIDE]
        spread = jnp.broadcast_to(own[None], (parts,) + own.shape)
        gathered.append(lax.all_to_all(spread, "kv", 0, 0, tiled=True).reshape(parts * rows, heads * WIDE))
    for c in range(CHUNKS):
        part = attend_call(c * heads, heads, lengths, gathered[c], prefix_keys, prefix_values, new_keys, new_values)
        part = lax.all_to_all(part.reshape(parts, rows, -1), "kv", 0, 0, tiled=True)
        results.append(merge_call(heads, parts, part.reshape(parts * rows, -1)))
    shift = [(s, (s + 1) % sections) for s in range(sections)]
    results = [lax.ppermute(r, "section", shift) for r in results]
    return jnp.concatenate(results, axis=1)


def solution(mesh):
    spread = P(("section", "kv"), None)
    return jax.shard_map(
        on_device,
        mesh=mesh,
        in_specs=(spread, spread, spread, spread, spread, P()),
        out_specs=spread,
        check_vma=False,
    )
```

time: 658 us -> 94.5 us (0.14)
  waiting for transfers between devices: 329 us -> 26.3 us
  other arithmetic: 114 us -> 0.66 us
  local copies, waits for them, and re-layouts: 77.7 us -> 8.68 us
  blocking collectives: 93 us -> 24.9 us
  matrix products: 25.5 us -> 0 us
  Pallas kernels: 0 us -> 22 us
  between operations: 13.6 us -> 0.13 us
  starting transfers between devices: 0.06 us -> 11.4 us
    all_gather x2 -> x0, waiting for transfers between devices: 323 us -> none  [the longest x1 280 us: joined(): pieces = jax.tree.map(lambda part: lax.all_gather(part, axis), value)]
    add x36 -> x0, other arithmetic: 102 us -> none  [the longest x15 101 us: join_pair(): left[0] * left_scale[..., None] + right[0] * right_scale[..., None]]
    all_gather x4 -> x0, blocking collectives: 93 us -> none  [the longest x2 47.5 us: joined(): pieces = jax.tree.map(lambda part: lax.all_gather(part, axis), value)]
    slice x6 -> x1, local copies, waits for them, and re-layouts: 45.4 us -> 0.88 us  [on_device(): own = queries[:, c * heads * WIDE:(c + 1) * heads * WIDE]]
    dot_general x10 -> x0, matrix products: 25.5 us -> none  [the longest x5 17 us: fold_block(): jnp.einsum('cjzm,mcv->cjzv', weights.astype(jnp.bfloat16), cached_value_b...]
    all_to_all x0 -> x1, blocking collectives: none -> 24.9 us  [on_device(): lax.all_to_all(spread, 'kv', 0, 0, tiled=True)]
    pallas_call x0 -> x4, Pallas kernels: none -> 22 us  [the longest x2 20.4 us: attend_call(): pl.pallas_call(functools.partial(attend, heads), grid=(heads,), in_specs=...]
    all_to_all x0 -> x3, waiting for transfers between devices: none -> 21.4 us  [the longest x2 18.5 us: on_device(): part = lax.all_to_all(part.reshape(parts, rows, -1), 'kv', 0, 0, tiled=True)]
  transfers between devices with their start and end apart: 3 -> 5, of which waited for: 3 -> 4; matrix products, arithmetic and copies ran while one was open for 1% -> 0% of each run, Pallas kernels for 0% -> 23%
where the time goes in v1:
time: 94.5 us; the launch traced here: 94 us
  waiting for transfers between devices  26.3 us (28%)
  blocking collectives  24.9 us (26%)
  Pallas kernels  22 us (23%)
  starting transfers between devices  11.4 us (12%)
  local copies, waits for them, and re-layouts  8.68 us (9%)
    all_to_all x1, blocking collectives, on_device(): lax.all_to_all(spread, 'kv', 0, 0, tiled=True)  24.9 us
    pallas_call x2, Pallas kernels, attend_call(): pl.pallas_call(functools.partial(attend, heads), grid=(heads,), in_specs=...  20.4 us
    all_to_all x2, waiting for transfers between devices, on_device(): part = lax.all_to_all(part.reshape(parts, rows, -1), 'kv', 0, 0, tiled=True)  18.5 us
    all_to_all x2, starting transfers between devices, on_device(): part = lax.all_to_all(part.reshape(parts, rows, -1), 'kv', 0, 0, tiled=True)  7.39 us
    unnamed x18, local copies, waits for them, and re-layouts  6.62 us
    ppermute x2, waiting for transfers between devices, on_device(): results = [lax.ppermute(r, 'section', shift) for r in results]  4.88 us
    all_to_all x1, starting transfers between devices, on_device(): lax.all_to_all(spread, 'kv', 0, 0, tiled=True)  3.98 us
    all_to_all x1, waiting for transfers between devices, on_device(): lax.all_to_all(spread, 'kv', 0, 0, tiled=True)  2.87 us
  transfers between devices with their start and end apart: 5, of which 4 were waited for; matrix products, arithmetic and copies ran while one was open for 0% of the time, Pallas kernels for 23%

profile of v1, /device:TPU:0, one launch (start us, length us, event | category | flops | bytes accessed | tf_op | source)
XLA Modules:
  0.0 94.0 jit_solution(11451928077613974377)
XLA Ops:
  0.0 0.9 fusion
  0.9 0.1 broadcast_in_dim.4
  1.0 24.9 %all_to_all.20 = bf16[16,8,4096]{2,1,0:T(8,128)(2,1)} all-to-all(bf16[16,8,4096]{2,1,0:T(8,128)(2,1)S(1)} %broadcast_in_dim.4), channel_id=1, replica_groups=mesh['section'=8,'kv'=16] {'kv'}, dimensions={0} | all-to-all | bytes 2097152 | tf_op jit(solution)/shard_map/all_to_all | solution.py:155
  25.9 0.0 copy-start.6
  25.9 0.0 copy-start.7
  25.9 1.1 %broadcast_in_dim.5 = bf16[16,8,4096]{2,1,0:T(8,128)(2,1)} broadcast(bf16[8,4096]{1,0:T(8,128)(2,1)S(1)} %get-tuple-element.6), dimensions={1,2} | broadcast | bytes 1114112 | tf_op jit(solution)/shard_map/broadcast_in_dim | solution.py:154
  27.0 0.0 copy-start
  27.0 0.0 copy-start.8
  27.0 4.0 %all-to-all-start.2 = ((bf16[16,8,4096]{2,1,0:T(8,128)(2,1)}), bf16[16,8,4096]{2,1,0:T(8,128)(2,1)S(1)}, u32[]{:S(2)}, u32[]{:S(2)}) async-start(bf16[16,8,4096]{2,1,0:T(8,128)(2,1)} %broadcast_in_dim.5), calls=%async_computation.2 | async-start | bytes 2097152 | tf_op jit(solution)/shard_map/all_to_all | solution.py:155
  30.9 0.0 copy-done.6
  31.0 0.0 copy-done.7
  31.0 0.0 copy-done
  31.0 0.0 copy-done.8
  31.0 0.0 copy-start.1
  31.0 1.6 %copy-done.1 = bf16[1024,1024]{1,0:T(8,128)(2,1)S(1)} copy-done((bf16[1024,1024]{1,0:T(8,128)(2,1)S(1)}, bf16[1024,1024]{1,0:T(8,128)(2,1)}, u32[]{:S(2)}) %copy-start.1) | copy-done | bytes 2097176
  32.6 0.0 copy-start.5
  32.6 1.2 %copy-done.5 = bf16[16,8,4096]{2,1,0:T(8,128)(2,1)S(1)} copy-done((bf16[16,8,4096]{2,1,0:T(8,128)(2,1)S(1)}, bf16[16,8,4096]{2,1,0:T(8,128)(2,1)}, u32[]{:S(2)}) %copy-start.5) | copy-done | bytes 1048600
  33.8 10.2 %attend.2 = bf16[128,4224]{1,0:T(8,128)(2,1)} custom-call(s32[8]{0:T(128)S(1)} %copy-done.8, bf16[128,4096]{1,0:T(8,128)(2,1)S(1)} %bitcast.9, bf16[1024,1024]{1,0:T(8,128)(2,1)S(1)} %copy-done, bf16[1024,1024]{1,0:T(8,128)(2,1)S(1)} %copy-done.1, bf16[8,1024]{1,0:T(8,128)(2,1)S(1)} %copy-done.6, bf16[8,1024]{1,0:T(8,128)(2,1)S(1)} %copy-done.7), custom_call_target="tpu_custom_call" | custom-call | tf_op jit(solution)/shard_map/attend/pallas_call | solution.py:102
  44.0 2.9 %all-to-all-done.2 = bf16[16,8,4096]{2,1,0:T(8,128)(2,1)S(1)} async-done(((bf16[16,8,4096]{2,1,0:T(8,128)(2,1)}), bf16[16,8,4096]{2,1,0:T(8,128)(2,1)S(1)}, u32[]{:S(2)}, u32[]{:S(2)}) %all-to-all-start.2) | async-done | bytes 1048608 | tf_op jit(solution)/shard_map/all_to_all | solution.py:155
  46.9 0.0 copy-start.3
  46.9 1.0 %copy-done.3 = bf16[16,8,4096]{2,1,0:T(8,128)(2,1)} copy-done((bf16[16,8,4096]{2,1,0:T(8,128)(2,1)}, bf16[16,8,4096]{2,1,0:T(8,128)(2,1)S(1)}, u32[]{:S(2)}) %copy-start.3) | copy-done | bytes 1048600
  47.9 3.7 %all-to-all-start.1 = ((bf16[16,8,4224]{2,1,0:T(8,128)(2,1)}), bf16[16,8,4224]{2,1,0:T(8,128)(2,1)S(1)}, u32[]{:S(2)}, u32[]{:S(2)}) async-start(bf16[16,8,4224]{2,1,0:T(8,128)(2,1)} %bitcast.1), calls=%async_computation.1 | async-start | bytes 2162688 | tf_op jit(solution)/shard_map/all_to_all | solution.py:158
  51.6 0.0 copy-start.2
  51.6 1.6 %copy-done.2 = bf16[1024,1024]{1,0:T(8,128)(2,1)S(1)} copy-done((bf16[1024,1024]{1,0:T(8,128)(2,1)S(1)}, bf16[1024,1024]{1,0:T(8,128)(2,1)}, u32[]{:S(2)}) %copy-start.2) | copy-done | bytes 2097176
  53.2 0.0 copy-start.4
  53.2 1.2 %copy-done.4 = bf16[16,8,4096]{2,1,0:T(8,128)(2,1)S(1)} copy-done((bf16[16,8,4096]{2,1,0:T(8,128)(2,1)S(1)}, bf16[16,8,4096]{2,1,0:T(8,128)(2,1)}, u32[]{:S(2)}) %copy-start.4) | copy-done | bytes 1048600
  54.4 10.2 %attend.3 = bf16[128,4224]{1,0:T(8,128)(2,1)} custom-call(s32[8]{0:T(128)S(1)} %copy-done.8, bf16[128,4096]{1,0:T(8,128)(2,1)S(1)} %bitcast.8, bf16[1024,1024]{1,0:T(8,128)(2,1)S(1)} %copy-done, bf16[1024,1024]{1,0:T(8,128)(2,1)S(1)} %copy-done.2, bf16[8,1024]{1,0:T(8,128)(2,1)S(1)} %copy-done.6, bf16[8,1024]{1,0:T(8,128)(2,1)S(1)} %copy-done.7), custom_call_target="tpu_custom_call" | custom-call | tf_op jit(solution)/shard_map/attend/pallas_call | solution.py:102
  64.6 3.3 %all-to-all-done.1 = bf16[16,8,4224]{2,1,0:T(8,128)(2,1)S(1)} async-done(((bf16[16,8,4224]{2,1,0:T(8,128)(2,1)}), bf16[16,8,4224]{2,1,0:T(8,128)(2,1)S(1)}, u32[]{:S(2)}, u32[]{:S(2)}) %all-to-all-start.1) | async-done | bytes 1081376 | tf_op jit(solution)/shard_map/all_to_all | solution.py:158
  67.9 3.7 %all-to-all-start.3 = ((bf16[16,8,4224]{2,1,0:T(8,128)(2,1)}), bf16[16,8,4224]{2,1,0:T(8,128)(2,1)S(1)}, u32[]{:S(2)}, u32[]{:S(2)}) async-start(bf16[16,8,4224]{2,1,0:T(8,128)(2,1)} %bitcast.4), calls=%async_computation.3 | async-start | bytes 2162688 | tf_op jit(solution)/shard_map/all_to_all | solution.py:158
  71.6 0.8 merge.2
  72.4 0.0 collective-permute-start
  72.4 15.2 %all-to-all-done.3 = bf16[16,8,4224]{2,1,0:T(8,128)(2,1)S(1)} async-done(((bf16[16,8,4224]{2,1,0:T(8,128)(2,1)}), bf16[16,8,4224]{2,1,0:T(8,128)(2,1)S(1)}, u32[]{:S(2)}, u32[]{:S(2)}) %all-to-all-start.3) | async-done | bytes 1081376 | tf_op jit(solution)/shard_map/all_to_all | solution.py:158
  87.6 0.8 merge.3
  88.4 0.0 collective-permute-start.1
  88.4 0.0 collective-permute-done
  88.4 4.9 %collective-permute-done.1 = bf16[8,4096]{1,0:T(8,128)(2,1)S(1)} collective-permute-done((bf16[8,4096]{1,0:T(8,128)(2,1)S(1)}, bf16[8,4096]{1,0:T(8,128)(2,1)S(1)}, u32[]{:S(2)}, u32[]{:S(2)}) %collective-permute-start.1) | collective-permute-done | bytes 65568 | tf_op jit(solution)/shard_map/ppermute | solution.py:161
  93.3 0.7 pad_maximum_fusion
Async XLA Ops:
  25.9 5.1 %copy-start.6 = (bf16[8,1024]{1,0:T(8,128)(2,1)S(1)}, bf16[8,1024]{1,0:T(8,128)(2,1)}, u32[]{:S(2)}) copy-start(bf16[8,1024]{1,0:T(8,128)(2,1)} %nk_ref.3) | copy-start | bytes 49156
  25.9 5.1 %copy-start.7 = (bf16[8,1024]{1,0:T(8,128)(2,1)S(1)}, bf16[8,1024]{1,0:T(8,128)(2,1)}, u32[]{:S(2)}) copy-start(bf16[8,1024]{1,0:T(8,128)(2,1)} %nv_ref.3) | copy-start | bytes 49156
  27.0 4.0 %copy-start = (bf16[1024,1024]{1,0:T(8,128)(2,1)S(1)}, bf16[1024,1024]{1,0:T(8,128)(2,1)}, u32[]{:S(2)}) copy-start(bf16[1024,1024]{1,0:T(8,128)(2,1)} %k_ref.3) | copy-start | bytes 6291460
  27.0 4.0 %copy-start.8 = (s32[8]{0:T(128)S(1)}, s32[8]{0:T(128)}, u32[]{:S(2)}) copy-start(s32[8]{0:T(128)} %lengths_ref.3) | copy-start | bytes 100
  27.0 19.9 %all-to-all-start.2 = ((bf16[16,8,4096]{2,1,0:T(8,128)(2,1)}), bf16[16,8,4096]{2,1,0:T(8,128)(2,1)S(1)}, u32[]{:S(2)}, u32[]{:S(2)}) async-start(bf16[16,8,4096]{2,1,0:T(8,128)(2,1)} %broadcast_in_dim.5), calls=%async_computation.2 | async-start | bytes 2097152 | tf_op jit(solution)/shard_map/all_to_all | solution.py:155
  31.0 1.6 %copy-start.1 = (bf16[1024,1024]{1,0:T(8,128)(2,1)S(1)}, bf16[1024,1024]{1,0:T(8,128)(2,1)}, u32[]{:S(2)}) copy-start(bf16[1024,1024]{1,0:T(8,128)(2,1)} %v_ref.3) | copy-start | bytes 6291460
  32.6 1.2 %copy-start.5 = (bf16[16,8,4096]{2,1,0:T(8,128)(2,1)S(1)}, bf16[16,8,4096]{2,1,0:T(8,128)(2,1)}, u32[]{:S(2)}) copy-start(bf16[16,8,4096]{2,1,0:T(8,128)(2,1)} %all_to_all.20) | copy-start | bytes 3145732
  46.9 1.0 %copy-start.3 = (bf16[16,8,4096]{2,1,0:T(8,128)(2,1)}, bf16[16,8,4096]{2,1,0:T(8,128)(2,1)S(1)}, u32[]{:S(2)}) copy-start(bf16[16,8,4096]{2,1,0:T(8,128)(2,1)S(1)} %all-to-all-done.2) | copy-start | bytes 3145732
  47.9 20.1 %all-to-all-start.1 = ((bf16[16,8,4224]{2,1,0:T(8,128)(2,1)}), bf16[16,8,4224]{2,1,0:T(8,128)(2,1)S(1)}, u32[]{:S(2)}, u32[]{:S(2)}) async-start(bf16[16,8,4224]{2,1,0:T(8,128)(2,1)} %bitcast.1), calls=%async_computation.1 | async-start | bytes 2162688 | tf_op jit(solution)/shard_map/all_to_all | solution.py:158
  51.6 1.6 %copy-start.2 = (bf16[1024,1024]{1,0:T(8,128)(2,1)S(1)}, bf16[1024,1024]{1,0:T(8,128)(2,1)}, u32[]{:S(2)}) copy-start(bf16[1024,1024]{1,0:T(8,128)(2,1)} %v_ref.3) | copy-start | bytes 6291460
  53.2 1.2 %copy-start.4 = (bf16[16,8,4096]{2,1,0:T(8,128)(2,1)S(1)}, bf16[16,8,4096]{2,1,0:T(8,128)(2,1)}, u32[]{:S(2)}) copy-start(bf16[16,8,4096]{2,1,0:T(8,128)(2,1)} %copy-done.3) | copy-start | bytes 3145732
  67.9 19.7 %all-to-all-start.3 = ((bf16[16,8,4224]{2,1,0:T(8,128)(2,1)}), bf16[16,8,4224]{2,1,0:T(8,128)(2,1)S(1)}, u32[]{:S(2)}, u32[]{:S(2)}) async-start(bf16[16,8,4224]{2,1,0:T(8,128)(2,1)} %bitcast.4), calls=%async_computation.3 | async-start | bytes 2162688 | tf_op jit(solution)/shard_map/all_to_all | solution.py:158
  72.4 16.0 %collective-permute-start = (bf16[8,4096]{1,0:T(8,128)(2,1)S(1)}, bf16[8,4096]{1,0:T(8,128)(2,1)S(1)}, u32[]{:S(2)}, u32[]{:S(2)}) collective-permute-start(bf16[8,4096]{1,0:T(8,128)(2,1)S(1)} %merge.2), channel_id=1, source_target_pairs={{0,16},{16,32},{32,48},{48,64},{64,80},{80,96},{96,112},{112,0},{1... | collective-permute-start | bytes 196616 | tf_op jit(solution)/shard_map/ppermute | solution.py:161
  88.4 4.9 %collective-permute-start.1 = (bf16[8,4096]{1,0:T(8,128)(2,1)S(1)}, bf16[8,4096]{1,0:T(8,128)(2,1)S(1)}, u32[]{:S(2)}, u32[]{:S(2)}) collective-permute-start(bf16[8,4096]{1,0:T(8,128)(2,1)S(1)} %merge.3), channel_id=1, source_target_pairs={{0,16},{16,32},{32,48},{48,64},{64,80},{80,96},{96,112},{112,0},{1... | collective-permute-start | bytes 196616 | tf_op jit(solution)/shard_map/ppermute | solution.py:161

commit v2 on v1

v2 whole, which is shorter than its diff:
```python
import functools

import jax
import jax.numpy as jnp
from jax import lax
from jax.experimental import pallas as pl
from jax.experimental.pallas import tpu as pltpu
from jax.sharding import PartitionSpec as P

H = 64
KVH = 8
DH = 128
GROUP = H // KVH
WIDE = GROUP * DH
SIDE = KVH // 2
AT_ONCE = 4

NEG = -1e30
FLOOR = -1e29
TINY = 1e-37
LOG2E = 1.4426950408889634
SENT = 2 * WIDE + 4 * DH
LEVELS = 2 * GROUP
STAGES = (((0, 0), (1, 0)), ((0, 1), (0, 3), (1, 1), (1, 3)), ((0, 2), (1, 2)))
MIB = 1024 * 1024
CUTS = 4


def contract(left, right, dim):
    return lax.dot_general(left, right, (((1,), (dim,)), ((), ())), preferred_element_type=jnp.float32)


def spread(q_ref, nk_ref, nv_ref, o_ref):
    rows = q_ref.shape[0]
    q, nk, nv = (ref[...].astype(jnp.float32) for ref in (q_ref, nk_ref, nv_ref))
    for pair in range(SIDE * SIDE // 2):
        both = []
        for target in (2 * pair, 2 * pair + 1):
            heads = (target % SIDE, SIDE + target // SIDE)
            pieces = [q[:, h * WIDE : (h + 1) * WIDE] for h in heads]
            pieces += [part[:, h * DH : (h + 1) * DH] for h in heads for part in (nk, nv)]
            both.append(jnp.concatenate(pieces, axis=1))
        o_ref[pair * 2 * rows : (pair + 1) * 2 * rows] = jnp.concatenate(both, axis=0).astype(jnp.bfloat16)


def spread_call(queries, new_keys, new_values):
    rows = queries.shape[0]
    return pl.pallas_call(
        spread,
        out_shape=jax.ShapeDtypeStruct((SIDE * SIDE * rows, SENT), jnp.bfloat16),
        compiler_params=pltpu.CompilerParams(vmem_limit_bytes=16 * MIB),
        name="spread",
    )(queries, new_keys, new_values)


def pack(moves, k_ref, v_ref, *refs):
    held, in_sems, out_sems = refs[-3:]
    depth = k_ref.shape[0]
    cut = depth // CUTS
    slot = lax.axis_index("kv")
    arriving = {}
    for c in range(CUTS):
        for i, ref in enumerate((k_ref, v_ref)):
            copy = pltpu.make_async_copy(ref.at[pl.ds(c * cut, cut)], held.at[i, pl.ds(c * cut, cut)], in_sems.at[2 * c + i])
            copy.start()
            arriving[c, i] = copy
    leaving = []
    for c in range(CUTS):
        for i in range(2):
            arriving[c, i].wait()
            for n, (line, step) in enumerate(moves):
                place = lax.rem(slot, SIDE) if line == 0 else lax.div(slot, SIDE)
                head = lax.rem(place + step, SIDE) + SIDE * line
                source = held.at[i, pl.ds(c * cut, cut), pl.ds(pl.multiple_of(head * DH, DH), DH)]
                target = refs[n].at[pl.ds(i * depth + c * cut, cut)]
                copy = pltpu.make_async_copy(source, target, out_sems.at[(2 * c + i) * len(moves) + n])
                copy.start()
                leaving.append(copy)
    for copy in leaving:
        copy.wait()


def pack_call(moves, keys, values):
    depth = keys.shape[0]
    return pl.pallas_call(
        functools.partial(pack, moves),
        in_specs=[pl.BlockSpec(memory_space=pl.ANY)] * 2,
        out_specs=[pl.BlockSpec(memory_space=pl.ANY)] * len(moves),
        out_shape=[jax.ShapeDtypeStruct((2 * depth, DH), jnp.bfloat16)] * len(moves),
        scratch_shapes=[
            pltpu.VMEM((2,) + keys.shape, jnp.bfloat16),
            pltpu.SemaphoreType.DMA((2 * CUTS,)),
            pltpu.SemaphoreType.DMA((2 * CUTS * len(moves),)),
        ],
        compiler_params=pltpu.CompilerParams(vmem_limit_bytes=60 * MIB),
        name="pack",
    )(keys, values)


def attend(moves, first, last, lengths_ref, q_ref, *refs):
    blocks, refs = refs[: len(moves)], refs[len(moves) :]
    rows = q_ref.shape[0]
    keys = blocks[0].shape[0] // 2
    slot = lax.axis_index("kv")
    length = lengths_ref[lax.axis_index("section")]
    place = (lax.rem(slot, SIDE), lax.div(slot, SIDE))
    scale = DH**-0.5 * LOG2E
    tall = rows * AT_ONCE
    places = lax.broadcasted_iota(jnp.int32, (1, keys), 1)
    lanes = lax.broadcasted_iota(jnp.int32, (rows, DH), 1)
    sides = []
    for line in range(2):
        mine = []
        if first:
            share = rows // SIDE
            low = place[1 - line] * share
            causal = lanes <= lax.broadcasted_iota(jnp.int32, (rows, DH), 0)
            own = jnp.logical_and(causal, jnp.logical_and(lanes >= low, lanes < low + share))
            own = jnp.concatenate([own] * AT_ONCE, axis=0)
            start = 2 * WIDE + 2 * line * DH
            mine.append((q_ref[:, start : start + DH], q_ref[:, start + DH : start + 2 * DH], own))
        for (way, step), ref in zip(moves, blocks):
            if way != line:
                continue
            back = lax.rem(place[line] + SIDE - step, SIDE)
            source = place[1] * SIDE + back if line == 0 else back * SIDE + place[0]
            mine.append((ref[:keys], ref[keys:], places < length - source * keys))
        sides.append([(k, jnp.concatenate([v, jnp.ones(v.shape, jnp.bfloat16)], axis=1), ok) for k, v, ok in mine])
    units = [(line, g, n) for line in range(2) for g in range(0, GROUP, AT_ONCE) for n in range(len(sides[line]))]

    def score(unit):
        line, g, n = unit
        columns = [q_ref[:, line * WIDE + (g + i) * DH : line * WIDE + (g + i + 1) * DH] for i in range(AT_ONCE)]
        return contract(jnp.concatenate(columns, axis=0), sides[line][n][0], 1)

    if last:
        (o_ref,) = refs if first else refs[2:]
        levels = jnp.full((rows, DH), FLOOR, jnp.float32)
    else:
        acc_out, peak_out = refs if first else refs[2:]
    s = score(units[0])
    for u, (line, g, n) in enumerate(units):
        following = score(units[u + 1]) if u + 1 < len(units) else None
        at = pl.ds((line * GROUP + g) * rows, tall)
        _, v, ok = sides[line][n]
        s = jnp.where(ok, s, NEG)
        top = jnp.broadcast_to(jnp.max(s, axis=1, keepdims=True) * scale, (tall, DH))
        if n == 0:
            old = None if first else refs[1][at]
            acc = None if first else refs[0][at]
        else:
            old = peak
        peak = jnp.maximum(top, FLOOR if old is None else old)
        w = jnp.exp2(s * scale - jnp.concatenate([peak] * (s.shape[1] // DH), axis=1)).astype(jnp.bfloat16)
        new = contract(w, v, 0)
        if old is None:
            acc = new
        else:
            factor = jnp.exp2(old - peak)
            acc = acc * jnp.concatenate([factor, factor], axis=1) + new
        if n == len(sides[line]) - 1:
            if last:
                total = jnp.maximum(acc[:, DH:], TINY)
                out = (acc[:, :DH] / total).astype(jnp.bfloat16)
                level = peak + jnp.log2(total)
                for i in range(AT_ONCE):
                    index = line * GROUP + g + i
                    o_ref[:, index * DH : (index + 1) * DH] = out[i * rows : (i + 1) * rows]
                    levels = jnp.where(lax.rem(lanes, LEVELS) == index, level[i * rows : (i + 1) * rows], levels)
            else:
                acc_out[at] = acc
                peak_out[at] = peak
        s = following
    if last:
        high = levels.astype(jnp.bfloat16).astype(jnp.float32)
        middle = (levels - high).astype(jnp.bfloat16).astype(jnp.float32)
        low = levels - high - middle
        picked = jnp.where(lanes < LEVELS, high, jnp.where(lanes < 2 * LEVELS, middle, low))
        o_ref[:, 2 * WIDE :] = picked.astype(jnp.bfloat16)


def attend_call(moves, lengths, q, blocks, state, last):
    rows = q.shape[0]
    if last:
        shapes = [jax.ShapeDtypeStruct((rows, 2 * WIDE + DH), jnp.bfloat16)]
    else:
        shapes = [jax.ShapeDtypeStruct((2 * GROUP * rows, width), jnp.float32) for width in (2 * DH, DH)]
    whole = pl.BlockSpec(memory_space=pltpu.VMEM)
    count = len(blocks) + len(state)
    return pl.pallas_call(
        functools.partial(attend, moves, not state, last),
        in_specs=[pl.BlockSpec(memory_space=pltpu.SMEM)] + [whole] * (1 + count),
        out_specs=[whole] * len(shapes),
        out_shape=shapes,
        compiler_params=pltpu.CompilerParams(vmem_limit_bytes=28 * MIB),
        name="attend",
    )(lengths, q, *blocks, *state)


def merge(x_ref, o_ref):
    rows = o_ref.shape[0]
    parts = SIDE * SIDE
    packed = x_ref[:, 2 * WIDE :].astype(jnp.float32).reshape(parts, rows, DH)
    level = packed[:, :, :LEVELS] + packed[:, :, LEVELS : 2 * LEVELS] + packed[:, :, 2 * LEVELS : 3 * LEVELS]
    level = [level[s] for s in range(parts)]
    upper = lax.broadcasted_iota(jnp.int32, (rows, LEVELS), 1) >= GROUP

    def shares(line):
        weights = [None] * parts
        for h in range(SIDE):
            group = [i * SIDE + h if line == 0 else h * SIDE + i for i in range(SIDE)]
            peak = functools.reduce(jnp.maximum, [level[s] for s in group])
            raised = [jnp.exp2(level[s] - peak) for s in group]
            total = sum(raised)
            for s, w in zip(group, raised):
                weights[s] = w / total
        return weights

    weights = [jnp.where(upper, high, low) for low, high in zip(shares(0), shares(1))]
    for line in range(2):
        for g in range(GROUP):
            index = line * GROUP + g
            x = x_ref[:, index * DH : (index + 1) * DH].astype(jnp.float32).reshape(parts, rows, DH)
            x = [x[s] * weights[s][:, index : index + 1] for s in range(parts)]
            for h in range(SIDE):
                group = [i * SIDE + h if line == 0 else h * SIDE + i for i in range(SIDE)]
                start = ((line * SIDE + h) * GROUP + g) * DH
                o_ref[:, start : start + DH] = sum(x[s] for s in group).astype(jnp.bfloat16)


def merge_call(x):
    return pl.pallas_call(
        merge,
        out_shape=jax.ShapeDtypeStruct((x.shape[0] // SIDE**2, H * DH), jnp.bfloat16),
        compiler_params=pltpu.CompilerParams(vmem_limit_bytes=16 * MIB),
        name="merge",
    )(x)


def on_device(queries, new_keys, new_values, prefix_keys, prefix_values, lengths):
    parts = lax.axis_size("kv")
    sections = lax.axis_size("section")
    rows = queries.shape[0]
    sent = spread_call(queries, new_keys, new_values)
    q = lax.all_to_all(sent.reshape(parts, rows, SENT), "kv", 0, 0, tiled=True).reshape(parts * rows, SENT)
    moves = [move for stage in STAGES for move in stage]
    far = [move for move in moves if move[1]]
    near = [move for move in moves if not move[1]]
    blocks = {}
    for move, block in zip(far + near, pack_call(far + near, prefix_keys, prefix_values)):
        line, step = move
        if step:
            pairs = []
            for a in range(SIDE):
                for b in range(SIDE):
                    to = (b + step) % SIDE
                    pairs.append((a * SIDE + b, a * SIDE + to) if line == 0 else (b * SIDE + a, to * SIDE + a))
            block = lax.ppermute(block, "kv", pairs)
        blocks[move] = block
    state = []
    for n, stage in enumerate(STAGES):
        state = attend_call(stage, lengths, q, [blocks[move] for move in stage], state, n == len(STAGES) - 1)
    part = lax.all_to_all(state[0].reshape(parts, rows, -1), "kv", 0, 0, tiled=True)
    merged = merge_call(part.reshape(parts * rows, -1))
    return lax.ppermute(merged, "section", [(s, (s + 1) % sections) for s in range(sections)])


def solution(mesh):
    split = P(("section", "kv"), None)
    return jax.shard_map(
        on_device,
        mesh=mesh,
        in_specs=(split, split, split, split, split, P()),
        out_specs=split,
        check_vma=False,
    )
```

time: 94.5 us -> 79.3 us (0.84)
  waiting for transfers between devices: 26.3 us -> 14.1 us
  starting transfers between devices: 11.4 us -> 21.9 us
  local copies, waits for them, and re-layouts: 8.68 us -> 1.71 us
  blocking collectives: 24.9 us -> 19.9 us
    all_to_all x3 -> x1, waiting for transfers between devices: 21.4 us -> 0.01 us  [on_device(): lax.all_to_all(sent.reshape(parts, rows, SENT), 'kv', 0, 0, tiled=True)]
    ppermute x2 -> x7, starting transfers between devices: 0.03 us -> 14.3 us  [the longest x6 14.3 us: on_device(): block = lax.ppermute(block, 'kv', pairs)]
    ppermute x2 -> x7, waiting for transfers between devices: 4.88 us -> 14.1 us  [the longest x6 8.51 us: on_device(): block = lax.ppermute(block, 'kv', pairs)]
    all_to_all x1, blocking collectives: 24.9 us -> 19.9 us  [on_device(): lax.all_to_all(state[0].reshape(parts, rows, -1), 'kv', 0, 0, tiled=True)]
    unnamed x18 -> x13, local copies, waits for them, and re-layouts: 6.62 us -> 1.71 us
    all_to_all x3 -> x1, starting transfers between devices: 11.4 us -> 7.59 us  [on_device(): lax.all_to_all(sent.reshape(parts, rows, SENT), 'kv', 0, 0, tiled=True)]
    broadcast_in_dim x2 -> x0, local copies, waits for them, and re-layouts: 1.18 us -> none  [on_device(): spread = jnp.broadcast_to(own[None], (parts,) + own.shape)]
    pallas_call x4 -> x6, Pallas kernels: 22 us -> 21.3 us  [the longest x3 15.8 us: attend_call(): pl.pallas_call(functools.partial(attend, moves, not state, last), in_spec...]
  transfers between devices with their start and end apart: 5 -> 8, of which waited for: 4 -> 5; matrix products, arithmetic and copies ran while one was open for 0% -> 0% of each run, Pallas kernels for 23% -> 15%
where the time goes in v2:
time: 79.3 us; the launch traced here: 79 us
  starting transfers between devices  21.9 us (28%)
  Pallas kernels  21.3 us (27%)
  blocking collectives  19.9 us (25%)
  waiting for transfers between devices  14.1 us (18%)
  local copies, waits for them, and re-layouts  1.71 us (2%)
    all_to_all x1, blocking collectives, on_device(): lax.all_to_all(state[0].reshape(parts, rows, -1), 'kv', 0, 0, tiled=True)  19.9 us
    pallas_call x3, Pallas kernels, attend_call(): pl.pallas_call(functools.partial(attend, moves, not state, last), in_spec...  15.8 us
    ppermute x6, starting transfers between devices, on_device(): block = lax.ppermute(block, 'kv', pairs)  14.3 us
    ppermute x6, waiting for transfers between devices, on_device(): block = lax.ppermute(block, 'kv', pairs)  8.51 us
    all_to_all x1, starting transfers between devices, on_device(): lax.all_to_all(sent.reshape(parts, rows, SENT), 'kv', 0, 0, tiled=True)  7.59 us
    ppermute x1, waiting for transfers between devices, on_device(): lax.ppermute(merged, 'section', [(s, (s + 1) % sections) for s in range(s...  5.59 us
    pallas_call x1, Pallas kernels, pack_call(): pl.pallas_call(functools.partial(pack, moves), in_specs=[pl.BlockSpec(mem...  4.13 us
    unnamed x13, local copies, waits for them, and re-layouts  1.71 us
  transfers between devices with their start and end apart: 8, of which 5 were waited for; matrix products, arithmetic and copies ran while one was open for 0% of the time, Pallas kernels for 15%

profile of v2, /device:TPU:0, one launch (start us, length us, event | category | flops | bytes accessed | tf_op | source)
XLA Modules:
  0.0 79.0 jit_solution(10931092914047832357)
XLA Ops:
  0.0 0.0 copy-start.4
  0.0 0.0 copy-start.3
  0.0 0.0 copy-start.2
  0.0 4.1 %pack.1 = (bf16[2048,128]{1,0:T(8,128)(2,1)}, bf16[2048,128]{1,0:T(8,128)(2,1)}, bf16[2048,128]{1,0:T(8,128)(2,1)}, bf16[2048,128]{1,0:T(8,128)(2,1)}, bf16[2048...) custom-call(bf16[1024,1024]{1,0:T(8,128)(2,1)} %k_ref.1, ...), custom_call_target="tpu_custom_call" | custom-call | tf_op jit(solution)/shard_map/pack/pallas_call | solution.py:85
  4.1 0.0 copy-start
  4.2 0.0 copy-start.5
  4.2 2.1 %collective-permute-start.2 = (bf16[2048,128]{1,0:T(8,128)(2,1)}, bf16[2048,128]{1,0:T(8,128)(2,1)S(1)}, u32[]{:S(2)}, u32[]{:S(2)}) collective-permute-start(bf16[2048,128]{1,0:T(8,128)(2,1)} %get-tuple-element.19), channel_id=1, source_target_pairs={{0,1},{1,2},{2,3},{3,0},{4,5},{5,6},{6,7},{7,4},{8,9},{9,10},{10,1... | collective-permute-start | bytes 1572872 | tf_op jit(solution)/shard_map/ppermute | solution.py:258
  6.2 0.0 copy-done.4
  6.2 0.0 copy-done.3
  6.3 0.0 copy-done.2
  6.3 0.9 %spread.1 = bf16[128,2560]{1,0:T(8,128)(2,1)} custom-call(bf16[8,8192]{1,0:T(8,128)(2,1)S(1)} %copy-done.2, bf16[8,1024]{1,0:T(8,128)(2,1)S(1)} %copy-done.3, bf16[8,1024]{1,0:T(8,128)(2,1)S(1)} %copy-done.4), custom_call_target="tpu_custom_call" | custom-call | tf_op jit(solution)/shard_map/spread/pallas_call | solution.py:48
  7.1 7.6 %all-to-all-start = ((bf16[16,8,2560]{2,1,0:T(8,128)(2,1)}), bf16[16,8,2560]{2,1,0:T(8,128)(2,1)S(1)}, u32[]{:S(2)}, u32[]{:S(2)}) async-start(bf16[16,8,2560]{2,1,0:T(8,128)(2,1)} %bitcast), calls=%async_computation | async-start | bytes 1310720 | tf_op jit(solution)/shard_map/all_to_all | solution.py:245
  14.7 3.1 %collective-permute-start.3 = (bf16[2048,128]{1,0:T(8,128)(2,1)}, bf16[2048,128]{1,0:T(8,128)(2,1)S(1)}, u32[]{:S(2)}, u32[]{:S(2)}) collective-permute-start(bf16[2048,128]{1,0:T(8,128)(2,1)} %get-tuple-element.20), channel_id=1, source_target_pairs={{0,3},{1,0},{2,1},{3,2},{4,7},{5,4},{6,5},{7,6},{8,11},{9,8},{10,9... | collective-permute-start | bytes 1572872 | tf_op jit(solution)/shard_map/ppermute | solution.py:258
  17.9 1.5 %collective-permute-start.4 = (bf16[2048,128]{1,0:T(8,128)(2,1)}, bf16[2048,128]{1,0:T(8,128)(2,1)S(1)}, u32[]{:S(2)}, u32[]{:S(2)}) collective-permute-start(bf16[2048,128]{1,0:T(8,128)(2,1)} %get-tuple-element.21), channel_id=1, source_target_pairs={{0,4},{4,8},{8,12},{12,0},{1,5},{5,9},{9,13},{13,1},{2,6},{6,10},{... | collective-permute-start | bytes 1572872 | tf_op jit(solution)/shard_map/ppermute | solution.py:258
  19.3 1.8 %collective-permute-start.5 = (bf16[2048,128]{1,0:T(8,128)(2,1)}, bf16[2048,128]{1,0:T(8,128)(2,1)S(1)}, u32[]{:S(2)}, u32[]{:S(2)}) collective-permute-start(bf16[2048,128]{1,0:T(8,128)(2,1)} %get-tuple-element.22), channel_id=1, source_target_pairs={{0,12},{4,0},{8,4},{12,8},{1,13},{5,1},{9,5},{13,9},{2,14},{6,2},{... | collective-permute-start | bytes 1572872 | tf_op jit(solution)/shard_map/ppermute | solution.py:258
  21.1 0.9 %collective-permute-start = (bf16[2048,128]{1,0:T(8,128)(2,1)}, bf16[2048,128]{1,0:T(8,128)(2,1)}, u32[]{:S(2)}, u32[]{:S(2)}) collective-permute-start(bf16[2048,128]{1,0:T(8,128)(2,1)} %get-tuple-element.17), channel_id=1, source_target_pairs={{0,2},{1,3},{2,0},{3,1},{4,6},{5,7},{6,4},{7,5},{8,10},{9,11},{10,... | collective-permute-start | bytes 1572872 | tf_op jit(solution)/shard_map/ppermute | solution.py:258
  22.0 2.9 %collective-permute-done.2.refs_0_ = bf16[2048,128]{1,0:T(8,128)(2,1)S(1)} collective-permute-done((bf16[2048,128]{1,0:T(8,128)(2,1)}, bf16[2048,128]{1,0:T(8,128)(2,1)S(1)}, u32[]{:S(2)}, u32[]{:S(2)}) %collective-permute-start.2) | collective-permute-done | bytes 524320 | tf_op jit(solution)/shard_map/ppermute | solution.py:258
  24.9 5.0 %collective-permute-start.1 = (bf16[2048,128]{1,0:T(8,128)(2,1)}, bf16[2048,128]{1,0:T(8,128)(2,1)}, u32[]{:S(2)}, u32[]{:S(2)}) collective-permute-start(bf16[2048,128]{1,0:T(8,128)(2,1)} %get-tuple-element.18), channel_id=1, source_target_pairs={{0,8},{4,12},{8,0},{12,4},{1,9},{5,13},{9,1},{13,5},{2,10},{6,14},... | collective-permute-start | bytes 1572872 | tf_op jit(solution)/shard_map/ppermute | solution.py:258
  29.8 0.0 all-to-all-done
  29.8 0.0 copy-done
  29.8 0.0 copy-done.5
  29.9 0.0 copy-start.1
  29.9 1.0 %copy-done.1 = bf16[2048,128]{1,0:T(8,128)(2,1)S(1)} copy-done((bf16[2048,128]{1,0:T(8,128)(2,1)S(1)}, bf16[2048,128]{1,0:T(8,128)(2,1)}, u32[]{:S(2)}) %copy-start.1) | copy-done | bytes 524312
  30.9 4.3 %attend.3 = (f32[2048,256]{1,0:T(8,128)S(1)}, f32[2048,128]{1,0:T(8,128)S(1)}) custom-call(s32[8]{0:T(128)S(1)} %copy-done.5, bf16[128,2560]{1,0:T(8,128)(2,1)S(1)} %bitcast.4, bf16[2048,128]{1,0:T(8,128)(2,1)S(1)} %copy-done, bf16[2048,128]{1,0:T(8,128)(2,1)S(1)} %copy-done.1), custom_call_target="tpu_custom_call" | custom-call | tf_op jit(solution)/shard_map/attend/pallas_call | solution.py:190
  35.2 1.5 %collective-permute-done.3.refs_1_ = bf16[2048,128]{1,0:T(8,128)(2,1)S(1)} collective-permute-done((bf16[2048,128]{1,0:T(8,128)(2,1)}, bf16[2048,128]{1,0:T(8,128)(2,1)S(1)}, u32[]{:S(2)}, u32[]{:S(2)}) %collective-permute-start.3) | collective-permute-done | bytes 524320 | tf_op jit(solution)/shard_map/ppermute | solution.py:258
  36.7 0.9 %collective-permute-done.4.refs_2_ = bf16[2048,128]{1,0:T(8,128)(2,1)S(1)} collective-permute-done((bf16[2048,128]{1,0:T(8,128)(2,1)}, bf16[2048,128]{1,0:T(8,128)(2,1)S(1)}, u32[]{:S(2)}, u32[]{:S(2)}) %collective-permute-start.4) | collective-permute-done | bytes 524320 | tf_op jit(solution)/shard_map/ppermute | solution.py:258
  37.6 0.0 collective-permute-done.5.refs_3_
  37.6 7.0 %attend.4 = (f32[2048,256]{1,0:T(8,128)S(1)}, f32[2048,128]{1,0:T(8,128)S(1)}) custom-call(s32[8]{0:T(128)S(1)} %copy-done.5, bf16[128,2560]{1,0:T(8,128)(2,1)S(1)} %bitcast.5, bf16[2048,128]{1,0:T(8,128)(2,1)S(1)} %collective-permute-done.2.refs_0_, bf16[2048,128]{1,0:T(8,128)(2,1)S(1)} %collective-permute-done.3.refs_1_, ...), custom_call_target="tpu_custom_call" | custom-call | tf_op jit(solution)/shard_map/attend/pallas_call | solution.py:190
  44.6 0.0 collective-permute-done.refs_0_
  44.7 3.2 %collective-permute-done.1.refs_1_ = bf16[2048,128]{1,0:T(8,128)(2,1)} collective-permute-done((bf16[2048,128]{1,0:T(8,128)(2,1)}, bf16[2048,128]{1,0:T(8,128)(2,1)}, u32[]{:S(2)}, u32[]{:S(2)}) %collective-permute-start.1) | collective-permute-done | bytes 524320 | tf_op jit(solution)/shard_map/ppermute | solution.py:258
  47.9 4.5 %attend.5 = bf16[128,2176]{1,0:T(8,128)(2,1)S(1)} custom-call(s32[8]{0:T(128)S(1)} %copy-done.5, bf16[128,2560]{1,0:T(8,128)(2,1)S(1)} %bitcast.6, bf16[2048,128]{1,0:T(8,128)(2,1)} %collective-permute-done.refs_0_, bf16[2048,128]{1,0:T(8,128)(2,1)} %collective-permute-done.1.refs_1_, f32[2048,256]{1,0:T(8,128)S(1)} %get-tuple-element.27.refs_2_, ...), custom_call_target="tpu_custom_call" | custom-call | tf_op jit(solution)/shard_map/attend/pallas_call | solution.py:190
  52.4 19.9 %all_to_all.10 = bf16[16,8,2176]{2,1,0:T(8,128)(2,1)S(1)} all-to-all(bf16[16,8,2176]{2,1,0:T(8,128)(2,1)S(1)} %bitcast.8), channel_id=1, replica_groups=mesh['section'=8,'kv'=16] {'kv'}, dimensions={0} | all-to-all | bytes 1114112 | tf_op jit(solution)/shard_map/all_to_all | solution.py:263
  72.2 0.5 merge.1
  72.7 0.0 collective-permute-start.6
  72.8 5.6 %collective-permute-done.6 = bf16[8,8192]{1,0:T(8,128)(2,1)S(1)} collective-permute-done((bf16[8,8192]{1,0:T(8,128)(2,1)S(1)}, bf16[8,8192]{1,0:T(8,128)(2,1)S(1)}, u32[]{:S(2)}, u32[]{:S(2)}) %collective-permute-start.6) | collective-permute-done | bytes 131104 | tf_op jit(solution)/shard_map/ppermute | solution.py:265
  78.3 0.7 copy.8
Async XLA Ops:
  0.0 6.2 %copy-start.4 = (bf16[8,1024]{1,0:T(8,128)(2,1)S(1)}, bf16[8,1024]{1,0:T(8,128)(2,1)}, u32[]{:S(2)}) copy-start(bf16[8,1024]{1,0:T(8,128)(2,1)} %nv_ref.1) | copy-start | bytes 49156
  0.0 6.2 %copy-start.3 = (bf16[8,1024]{1,0:T(8,128)(2,1)S(1)}, bf16[8,1024]{1,0:T(8,128)(2,1)}, u32[]{:S(2)}) copy-start(bf16[8,1024]{1,0:T(8,128)(2,1)} %nk_ref.1) | copy-start | bytes 49156
  0.0 6.2 %copy-start.2 = (bf16[8,8192]{1,0:T(8,128)(2,1)S(1)}, bf16[8,8192]{1,0:T(8,128)(2,1)}, u32[]{:S(2)}) copy-start(bf16[8,8192]{1,0:T(8,128)(2,1)} %q_ref.1) | copy-start | bytes 393220
  4.1 25.7 %copy-start = (bf16[2048,128]{1,0:T(8,128)(2,1)S(1)}, bf16[2048,128]{1,0:T(8,128)(2,1)}, u32[]{:S(2)}) copy-start(bf16[2048,128]{1,0:T(8,128)(2,1)} %get-tuple-element.23.refs_0_) | copy-start | bytes 1572868
  4.2 25.7 %copy-start.5 = (s32[8]{0:T(128)S(1)}, s32[8]{0:T(128)}, u32[]{:S(2)}) copy-start(s32[8]{0:T(128)} %lengths_ref.5) | copy-start | bytes 100
  4.2 20.7 %collective-permute-start.2 = (bf16[2048,128]{1,0:T(8,128)(2,1)}, bf16[2048,128]{1,0:T(8,128)(2,1)S(1)}, u32[]{:S(2)}, u32[]{:S(2)}) collective-permute-start(bf16[2048,128]{1,0:T(8,128)(2,1)} %get-tuple-element.19), channel_id=1, source_target_pairs={{0,1},{1,2},{2,3},{3,0},{4,5},{5,6},{6,7},{7,4},{8,9},{9,10},{10,1... | collective-permute-start | bytes 1572872 | tf_op jit(solution)/shard_map/ppermute | solution.py:258
  7.1 22.7 %all-to-all-start = ((bf16[16,8,2560]{2,1,0:T(8,128)(2,1)}), bf16[16,8,2560]{2,1,0:T(8,128)(2,1)S(1)}, u32[]{:S(2)}, u32[]{:S(2)}) async-start(bf16[16,8,2560]{2,1,0:T(8,128)(2,1)} %bitcast), calls=%async_computation | async-start | bytes 1310720 | tf_op jit(solution)/shard_map/all_to_all | solution.py:245
  14.7 22.0 %collective-permute-start.3 = (bf16[2048,128]{1,0:T(8,128)(2,1)}, bf16[2048,128]{1,0:T(8,128)(2,1)S(1)}, u32[]{:S(2)}, u32[]{:S(2)}) collective-permute-start(bf16[2048,128]{1,0:T(8,128)(2,1)} %get-tuple-element.20), channel_id=1, source_target_pairs={{0,3},{1,0},{2,1},{3,2},{4,7},{5,4},{6,5},{7,6},{8,11},{9,8},{10,9... | collective-permute-start | bytes 1572872 | tf_op jit(solution)/shard_map/ppermute | solution.py:258
  17.9 19.7 %collective-permute-start.4 = (bf16[2048,128]{1,0:T(8,128)(2,1)}, bf16[2048,128]{1,0:T(8,128)(2,1)S(1)}, u32[]{:S(2)}, u32[]{:S(2)}) collective-permute-start(bf16[2048,128]{1,0:T(8,128)(2,1)} %get-tuple-element.21), channel_id=1, source_target_pairs={{0,4},{4,8},{8,12},{12,0},{1,5},{5,9},{9,13},{13,1},{2,6},{6,10},{... | collective-permute-start | bytes 1572872 | tf_op jit(solution)/shard_map/ppermute | solution.py:258
  19.3 18.3 %collective-permute-start.5 = (bf16[2048,128]{1,0:T(8,128)(2,1)}, bf16[2048,128]{1,0:T(8,128)(2,1)S(1)}, u32[]{:S(2)}, u32[]{:S(2)}) collective-permute-start(bf16[2048,128]{1,0:T(8,128)(2,1)} %get-tuple-element.22), channel_id=1, source_target_pairs={{0,12},{4,0},{8,4},{12,8},{1,13},{5,1},{9,5},{13,9},{2,14},{6,2},{... | collective-permute-start | bytes 1572872 | tf_op jit(solution)/shard_map/ppermute | solution.py:258
  21.1 23.5 %collective-permute-start = (bf16[2048,128]{1,0:T(8,128)(2,1)}, bf16[2048,128]{1,0:T(8,128)(2,1)}, u32[]{:S(2)}, u32[]{:S(2)}) collective-permute-start(bf16[2048,128]{1,0:T(8,128)(2,1)} %get-tuple-element.17), channel_id=1, source_target_pairs={{0,2},{1,3},{2,0},{3,1},{4,6},{5,7},{6,4},{7,5},{8,10},{9,11},{10,... | collective-permute-start | bytes 1572872 | tf_op jit(solution)/shard_map/ppermute | solution.py:258
  24.9 23.0 %collective-permute-start.1 = (bf16[2048,128]{1,0:T(8,128)(2,1)}, bf16[2048,128]{1,0:T(8,128)(2,1)}, u32[]{:S(2)}, u32[]{:S(2)}) collective-permute-start(bf16[2048,128]{1,0:T(8,128)(2,1)} %get-tuple-element.18), channel_id=1, source_target_pairs={{0,8},{4,12},{8,0},{12,4},{1,9},{5,13},{9,1},{13,5},{2,10},{6,14},... | collective-permute-start | bytes 1572872 | tf_op jit(solution)/shard_map/ppermute | solution.py:258
  29.9 1.0 %copy-start.1 = (bf16[2048,128]{1,0:T(8,128)(2,1)S(1)}, bf16[2048,128]{1,0:T(8,128)(2,1)}, u32[]{:S(2)}) copy-start(bf16[2048,128]{1,0:T(8,128)(2,1)} %get-tuple-element.24.refs_1_) | copy-start | bytes 1572868
  72.7 5.6 %collective-permute-start.6 = (bf16[8,8192]{1,0:T(8,128)(2,1)S(1)}, bf16[8,8192]{1,0:T(8,128)(2,1)S(1)}, u32[]{:S(2)}, u32[]{:S(2)}) collective-permute-start(bf16[8,8192]{1,0:T(8,128)(2,1)S(1)} %merge.1), channel_id=1, source_target_pairs={{0,16},{16,32},{32,48},{48,64},{64,80},{80,96},{96,112},{112,0},{1... | collective-permute-start | bytes 393224 | tf_op jit(solution)/shard_map/ppermute | solution.py:265

commit v3 on v2

--- a/solution.py
+++ b/solution.py
@@ -21,13 +21,24 @@
 LOG2E = 1.4426950408889634
 SENT = 2 * WIDE + 4 * DH
 LEVELS = 2 * GROUP
-STAGES = (((0, 0), (1, 0)), ((0, 1), (0, 3), (1, 1), (1, 3)), ((0, 2), (1, 2)))
+STAGES = (((0, 0), (1, 0)), ((0, 1), (0, 2), (1, 1), (1, 2)), ((0, 3), (1, 3)))
 MIB = 1024 * 1024
 CUTS = 4
 
 
 def contract(left, right, dim):
     return lax.dot_general(left, right, (((1,), (dim,)), ((), ())), preferred_element_type=jnp.float32)
+
+
+def member(slot):
+    return slot // SIDE % 2 * 2 + slot % 2
+
+
+def partner(slot, tiling, flip):
+    y, z = slot // SIDE, slot % SIDE
+    y = (((y + tiling) ^ flip // 2) - tiling) % SIDE
+    z = (((z + tiling) ^ flip % 2) - tiling) % SIDE
+    return y * SIDE + z
 
 
 def spread(q_ref, nk_ref, nv_ref, o_ref):
@@ -36,7 +47,7 @@
     for pair in range(SIDE * SIDE // 2):
         both = []
         for target in (2 * pair, 2 * pair + 1):
-            heads = (target % SIDE, SIDE + target // SIDE)
+            heads = (member(target), KVH - 1 - member(target))
             pieces = [q[:, h * WIDE : (h + 1) * WIDE] for h in heads]
             pieces += [part[:, h * DH : (h + 1) * DH] for h in heads for part in (nk, nv)]
             both.append(jnp.concatenate(pieces, axis=1))
@@ -48,7 +59,8 @@
     return pl.pallas_call(
         spread,
         out_shape=jax.ShapeDtypeStruct((SIDE * SIDE * rows, SENT), jnp.bfloat16),
-        compiler_params=pltpu.CompilerParams(vmem_limit_bytes=16 * MIB),
+        compiler_params=pltpu.CompilerParams(vmem_limit_bytes=60 * MIB),
+        cost_estimate=pl.CostEstimate(flops=100_000_000_000, bytes_accessed=0, transcendentals=0),
         name="spread",
     )(queries, new_keys, new_values)
 
@@ -68,9 +80,9 @@
     for c in range(CUTS):
         for i in range(2):
             arriving[c, i].wait()
-            for n, (line, step) in enumerate(moves):
-                place = lax.rem(slot, SIDE) if line == 0 else lax.div(slot, SIDE)
-                head = lax.rem(place + step, SIDE) + SIDE * line
+            for n, (tiling, flip) in enumerate(moves):
+                place = jnp.bitwise_xor(lax.rem(lax.div(slot, SIDE), 2) * 2 + lax.rem(slot, 2), flip)
+                head = KVH - 1 - place if tiling else place
                 source = held.at[i, pl.ds(c * cut, cut), pl.ds(pl.multiple_of(head * DH, DH), DH)]
                 target = refs[n].at[pl.ds(i * depth + c * cut, cut)]
                 copy = pltpu.make_async_copy(source, target, out_sems.at[(2 * c + i) * len(moves) + n])
@@ -92,7 +104,7 @@
             pltpu.SemaphoreType.DMA((2 * CUTS,)),
             pltpu.SemaphoreType.DMA((2 * CUTS * len(moves),)),
         ],
-        compiler_params=pltpu.CompilerParams(vmem_limit_bytes=60 * MIB),
+        compiler_params=pltpu.CompilerParams(vmem_limit_bytes=56 * MIB),
         name="pack",
     )(keys, values)
 
@@ -103,7 +115,7 @@
     keys = blocks[0].shape[0] // 2
     slot = lax.axis_index("kv")
     length = lengths_ref[lax.axis_index("section")]
-    place = (lax.rem(slot, SIDE), lax.div(slot, SIDE))
+    across = (lax.div(slot, SIDE), lax.rem(slot, SIDE))
     scale = DH**-0.5 * LOG2E
     tall = rows * AT_ONCE
     places = lax.broadcasted_iota(jnp.int32, (1, keys), 1)
@@ -113,17 +125,18 @@
         mine = []
         if first:
             share = rows // SIDE
-            low = place[1 - line] * share
+            low = (lax.div(across[0], 2) * 2 + lax.div(across[1], 2)) * share
             causal = lanes <= lax.broadcasted_iota(jnp.int32, (rows, DH), 0)
             own = jnp.logical_and(causal, jnp.logical_and(lanes >= low, lanes < low + share))
             own = jnp.concatenate([own] * AT_ONCE, axis=0)
             start = 2 * WIDE + 2 * line * DH
             mine.append((q_ref[:, start : start + DH], q_ref[:, start + DH : start + 2 * DH], own))
-        for (way, step), ref in zip(moves, blocks):
-            if way != line:
+        for (tiling, flip), ref in zip(moves, blocks):
+            if tiling != line:
                 continue
-            back = lax.rem(place[line] + SIDE - step, SIDE)
-            source = place[1] * SIDE + back if line == 0 else back * SIDE + place[0]
+            flips = (flip // 2, flip % 2)
+            y, z = (lax.rem(jnp.bitwise_xor(at + line, bit) - line + SIDE, SIDE) for at, bit in zip(across, flips))
+            source = y * SIDE + z
             mine.append((ref[:keys], ref[keys:], places < length - source * keys))
         sides.append([(k, jnp.concatenate([v, jnp.ones(v.shape, jnp.bfloat16)], axis=1), ok) for k, v, ok in mine])
     units = [(line, g, n) for line in range(2) for g in range(0, GROUP, AT_ONCE) for n in range(len(sides[line]))]
@@ -193,6 +206,7 @@
         out_specs=[whole] * len(shapes),
         out_shape=shapes,
         compiler_params=pltpu.CompilerParams(vmem_limit_bytes=28 * MIB),
+        cost_estimate=pl.CostEstimate(flops=0, bytes_accessed=0, transcendentals=0),
         name="attend",
     )(lengths, q, *blocks, *state)
 
@@ -203,28 +217,21 @@
     packed = x_ref[:, 2 * WIDE :].astype(jnp.float32).reshape(parts, rows, DH)
     level = packed[:, :, :LEVELS] + packed[:, :, LEVELS : 2 * LEVELS] + packed[:, :, 2 * LEVELS : 3 * LEVELS]
     level = [level[s] for s in range(parts)]
-    upper = lax.broadcasted_iota(jnp.int32, (rows, LEVELS), 1) >= GROUP
-
-    def shares(line):
-        weights = [None] * parts
-        for h in range(SIDE):
-            group = [i * SIDE + h if line == 0 else h * SIDE + i for i in range(SIDE)]
-            peak = functools.reduce(jnp.maximum, [level[s] for s in group])
-            raised = [jnp.exp2(level[s] - peak) for s in group]
-            total = sum(raised)
-            for s, w in zip(group, raised):
-                weights[s] = w / total
-        return weights
-
-    weights = [jnp.where(upper, high, low) for low, high in zip(shares(0), shares(1))]
+    groups = [[s for s in range(parts) if member(s) == h] for h in range(SIDE)]
+    weights = [None] * parts
+    for group in groups:
+        peak = functools.reduce(jnp.maximum, [level[s] for s in group])
+        raised = [jnp.exp2(level[s] - peak) for s in group]
+        total = sum(raised)
+        for s, w in zip(group, raised):
+            weights[s] = w / total
     for line in range(2):
         for g in range(GROUP):
             index = line * GROUP + g
             x = x_ref[:, index * DH : (index + 1) * DH].astype(jnp.float32).reshape(parts, rows, DH)
             x = [x[s] * weights[s][:, index : index + 1] for s in range(parts)]
-            for h in range(SIDE):
-                group = [i * SIDE + h if line == 0 else h * SIDE + i for i in range(SIDE)]
-                start = ((line * SIDE + h) * GROUP + g) * DH
+            for h, group in enumerate(groups):
+                start = ((KVH - 1 - h if line else h) * GROUP + g) * DH
                 o_ref[:, start : start + DH] = sum(x[s] for s in group).astype(jnp.bfloat16)
 
 
@@ -241,24 +248,24 @@
     parts = lax.axis_size("kv")
     sections = lax.axis_size("section")
     rows = queries.shape[0]
+    moves = [(tiling, flip) for flip in (1, 2, 3, 0) for tiling in range(2)]
+    packed = dict(zip(moves, pack_call(moves, prefix_keys, prefix_values)))
     sent = spread_call(queries, new_keys, new_values)
     q = lax.all_to_all(sent.reshape(parts, rows, SENT), "kv", 0, 0, tiled=True).reshape(parts * rows, SENT)
-    moves = [move for stage in STAGES for move in stage]
-    far = [move for move in moves if move[1]]
-    near = [move for move in moves if not move[1]]
-    blocks = {}
-    for move, block in zip(far + near, pack_call(far + near, prefix_keys, prefix_values)):
-        line, step = move
-        if step:
-            pairs = []
-            for a in range(SIDE):
-                for b in range(SIDE):
-                    to = (b + step) % SIDE
-                    pairs.append((a * SIDE + b, a * SIDE + to) if line == 0 else (b * SIDE + a, to * SIDE + a))
-            block = lax.ppermute(block, "kv", pairs)
-        blocks[move] = block
+    def travel(move, after):
+        block = packed[move]
+        if not move[1]:
+            return block
+        if after is not None:
+            block = lax.optimization_barrier((block, after))[0]
+        return lax.ppermute(block, "kv", [(s, partner(s, *move)) for s in range(parts)])
+
+    blocks = {move: travel(move, None) for move in moves if move[1] != 3}
+    arrived = [block for move, block in blocks.items() if move[1]]
     state = []
     for n, stage in enumerate(STAGES):
+        if n == 0:
+            blocks.update({move: travel(move, arrived) for move in moves if move[1] == 3})
         state = attend_call(stage, lengths, q, [blocks[move] for move in stage], state, n == len(STAGES) - 1)
     part = lax.all_to_all(state[0].reshape(parts, rows, -1), "kv", 0, 0, tiled=True)
     merged = merge_call(part.reshape(parts * rows, -1))

time: 79.3 us -> 73 us (0.921)
  starting transfers between devices: 21.9 us -> 15.9 us
  blocking collectives: 19.9 us -> 14.7 us
  waiting for transfers between devices: 14.1 us -> 18.7 us
    all_to_all x1, blocking collectives: 19.9 us -> 14.7 us  [on_device(): lax.all_to_all(state[0].reshape(parts, rows, -1), 'kv', 0, 0, tiled=True)]
    all_to_all x1, starting transfers between devices: 7.59 us -> 3.59 us  [on_device(): lax.all_to_all(sent.reshape(parts, rows, SENT), 'kv', 0, 0, tiled=True)]
    all_to_all x1, waiting for transfers between devices: 0.01 us -> 2.42 us  [on_device(): lax.all_to_all(sent.reshape(parts, rows, SENT), 'kv', 0, 0, tiled=True)]
    ppermute x6, waiting for transfers between devices: 8.51 us -> 10.7 us  [travel(): lax.ppermute(block, 'kv', [(s, partner(s, *move)) for s in range(parts)])]
    ppermute x6, starting transfers between devices: 14.3 us -> 12.2 us  [travel(): lax.ppermute(block, 'kv', [(s, partner(s, *move)) for s in range(parts)])]
    pallas_call x1, Pallas kernels: 0.89 us -> 1.81 us  [spread_call(): pl.pallas_call(spread, out_shape=jax.ShapeDtypeStruct((SIDE * SIDE * rows...]
    unnamed x13 -> x7, local copies, waits for them, and re-layouts: 1.71 us -> 1.71 us
  transfers between devices with their start and end apart: 8 -> 8, of which waited for: 5 -> 6; matrix products, arithmetic and copies ran while one was open for 0% -> 0% of each run, Pallas kernels for 15% -> 18%
where the time goes in v3:
time: 73 us; the launch traced here: 72.7 us
  Pallas kernels  21.7 us (30%)
  waiting for transfers between devices  18.7 us (26%)
  starting transfers between devices  15.9 us (22%)
  blocking collectives  14.7 us (20%)
  local copies, waits for them, and re-layouts  1.71 us (2%)
    pallas_call x3, Pallas kernels, attend_call(): pl.pallas_call(functools.partial(attend, moves, not state, last), in_spec...  15.3 us
    all_to_all x1, blocking collectives, on_device(): lax.all_to_all(state[0].reshape(parts, rows, -1), 'kv', 0, 0, tiled=True)  14.7 us
    ppermute x6, starting transfers between devices, travel(): lax.ppermute(block, 'kv', [(s, partner(s, *move)) for s in range(parts)])  12.2 us
    ppermute x6, waiting for transfers between devices, travel(): lax.ppermute(block, 'kv', [(s, partner(s, *move)) for s in range(parts)])  10.7 us
    ppermute x1, waiting for transfers between devices, on_device(): lax.ppermute(merged, 'section', [(s, (s + 1) % sections) for s in range(s...  5.59 us
    pallas_call x1, Pallas kernels, pack_call(): pl.pallas_call(functools.partial(pack, moves), in_specs=[pl.BlockSpec(mem...  4.12 us
    all_to_all x1, starting transfers between devices, on_device(): lax.all_to_all(sent.reshape(parts, rows, SENT), 'kv', 0, 0, tiled=True)  3.59 us
    all_to_all x1, waiting for transfers between devices, on_device(): lax.all_to_all(sent.reshape(parts, rows, SENT), 'kv', 0, 0, tiled=True)  2.42 us
  transfers between devices with their start and end apart: 8, of which 6 were waited for; matrix products, arithmetic and copies ran while one was open for 0% of the time, Pallas kernels for 18%

profile of v3, /device:TPU:0, one launch (start us, length us, event | category | flops | bytes accessed | tf_op | source)
XLA Modules:
  0.0 72.7 jit_solution(15161332326425518924)
XLA Ops:
  0.0 4.1 %pack.1 = (bf16[2048,128]{1,0:T(8,128)(2,1)}, bf16[2048,128]{1,0:T(8,128)(2,1)}, bf16[2048,128]{1,0:T(8,128)(2,1)}, bf16[2048,128]{1,0:T(8,128)(2,1)}, bf16[2048...) custom-call(bf16[1024,1024]{1,0:T(8,128)(2,1)} %k_ref.1, ...), custom_call_target="tpu_custom_call" | custom-call | tf_op jit(solution)/shard_map/pack/pallas_call | solution.py:97
  4.1 2.1 %collective-permute-start = (bf16[2048,128]{1,0:T(8,128)(2,1)}, bf16[2048,128]{1,0:T(8,128)(2,1)S(1)}, u32[]{:S(2)}, u32[]{:S(2)}) collective-permute-start(bf16[2048,128]{1,0:T(8,128)(2,1)} %get-tuple-element.20), channel_id=1, source_target_pairs={{0,1},{1,0},{2,3},{3,2},{4,5},{5,4},{6,7},{7,6},{8,9},{9,8},{10,11... | collective-permute-start | bytes 1572872 | tf_op jit(solution)/shard_map/ppermute | solution.py:261
  6.2 2.5 %collective-permute-start.1 = (bf16[2048,128]{1,0:T(8,128)(2,1)}, bf16[2048,128]{1,0:T(8,128)(2,1)S(1)}, u32[]{:S(2)}, u32[]{:S(2)}) collective-permute-start(bf16[2048,128]{1,0:T(8,128)(2,1)} %get-tuple-element.21), channel_id=1, source_target_pairs={{0,3},{1,2},{2,1},{3,0},{4,7},{5,6},{6,5},{7,4},{8,11},{9,10},{10,... | collective-permute-start | bytes 1572872 | tf_op jit(solution)/shard_map/ppermute | solution.py:261
  8.7 1.6 %collective-permute-start.2 = (bf16[2048,128]{1,0:T(8,128)(2,1)}, bf16[2048,128]{1,0:T(8,128)(2,1)S(1)}, u32[]{:S(2)}, u32[]{:S(2)}) collective-permute-start(bf16[2048,128]{1,0:T(8,128)(2,1)} %get-tuple-element.22), channel_id=1, source_target_pairs={{0,4},{1,5},{2,6},{3,7},{4,0},{5,1},{6,2},{7,3},{8,12},{9,13},{10,... | collective-permute-start | bytes 1572872 | tf_op jit(solution)/shard_map/ppermute | solution.py:261
  10.3 0.0 copy-start
  10.3 0.0 copy-start.2
  10.3 2.2 %collective-permute-start.3 = (bf16[2048,128]{1,0:T(8,128)(2,1)}, bf16[2048,128]{1,0:T(8,128)(2,1)S(1)}, u32[]{:S(2)}, u32[]{:S(2)}) collective-permute-start(bf16[2048,128]{1,0:T(8,128)(2,1)} %get-tuple-element.23), channel_id=1, source_target_pairs={{0,12},{1,13},{2,14},{3,15},{4,8},{5,9},{6,10},{7,11},{8,4},{9,5},... | collective-permute-start | bytes 1572872 | tf_op jit(solution)/shard_map/ppermute | solution.py:261
  12.5 1.8 %spread.1 = bf16[128,2560]{1,0:T(8,128)(2,1)} custom-call(bf16[8,8192]{1,0:T(8,128)(2,1)} %q_ref.1, bf16[8,1024]{1,0:T(8,128)(2,1)} %nk_ref.1, bf16[8,1024]{1,0:T(8,128)(2,1)} %nv_ref.1), custom_call_target="tpu_custom_call" | custom-call | flops 99999997952 | tf_op jit(solution)/shard_map/spread/pallas_call | solution.py:59
  14.3 3.6 %all-to-all-start = ((bf16[16,8,2560]{2,1,0:T(8,128)(2,1)}), bf16[16,8,2560]{2,1,0:T(8,128)(2,1)S(1)}, u32[]{:S(2)}, u32[]{:S(2)}) async-start(bf16[16,8,2560]{2,1,0:T(8,128)(2,1)} %bitcast.9), calls=%async_computation | async-start | bytes 1310720 | tf_op jit(solution)/shard_map/all_to_all | solution.py:254
  17.9 0.4 collective-permute-done.refs_0_
  18.3 3.5 %collective-permute-done.1.refs_2_ = bf16[2048,128]{1,0:T(8,128)(2,1)S(1)} collective-permute-done((bf16[2048,128]{1,0:T(8,128)(2,1)}, bf16[2048,128]{1,0:T(8,128)(2,1)S(1)}, u32[]{:S(2)}, u32[]{:S(2)}) %collective-permute-start.1) | collective-permute-done | bytes 524320 | tf_op jit(solution)/shard_map/ppermute | solution.py:261
  21.9 1.9 %collective-permute-done.2.refs_1_ = bf16[2048,128]{1,0:T(8,128)(2,1)S(1)} collective-permute-done((bf16[2048,128]{1,0:T(8,128)(2,1)}, bf16[2048,128]{1,0:T(8,128)(2,1)S(1)}, u32[]{:S(2)}, u32[]{:S(2)}) %collective-permute-start.2) | collective-permute-done | bytes 524320 | tf_op jit(solution)/shard_map/ppermute | solution.py:261
  23.8 4.8 %collective-permute-done.3.refs_3_ = bf16[2048,128]{1,0:T(8,128)(2,1)S(1)} collective-permute-done((bf16[2048,128]{1,0:T(8,128)(2,1)}, bf16[2048,128]{1,0:T(8,128)(2,1)S(1)}, u32[]{:S(2)}, u32[]{:S(2)}) %collective-permute-start.3) | collective-permute-done | bytes 524320 | tf_op jit(solution)/shard_map/ppermute | solution.py:261
  28.6 0.8 %collective-permute-start.4 = (bf16[2048,128]{1,0:T(8,128)(2,1)}, bf16[2048,128]{1,0:T(8,128)(2,1)}, u32[]{:S(2)}, u32[]{:S(2)}) collective-permute-start(bf16[2048,128]{1,0:T(8,128)(2,1)} %get-tuple-element.24), channel_id=1, source_target_pairs={{0,5},{1,4},{2,7},{3,6},{4,1},{5,0},{6,3},{7,2},{8,13},{9,12},{10,... | collective-permute-start | bytes 1572872 | tf_op jit(solution)/shard_map/ppermute | solution.py:261
  29.3 3.1 %collective-permute-start.5 = (bf16[2048,128]{1,0:T(8,128)(2,1)}, bf16[2048,128]{1,0:T(8,128)(2,1)}, u32[]{:S(2)}, u32[]{:S(2)}) collective-permute-start(bf16[2048,128]{1,0:T(8,128)(2,1)} %get-tuple-element.26), channel_id=1, source_target_pairs={{0,15},{1,14},{2,13},{3,12},{4,11},{5,10},{6,9},{7,8},{8,7},{9,6},... | collective-permute-start | bytes 1572872 | tf_op jit(solution)/shard_map/ppermute | solution.py:261
  32.4 2.4 %all-to-all-done = bf16[16,8,2560]{2,1,0:T(8,128)(2,1)S(1)} async-done(((bf16[16,8,2560]{2,1,0:T(8,128)(2,1)}), bf16[16,8,2560]{2,1,0:T(8,128)(2,1)S(1)}, u32[]{:S(2)}, u32[]{:S(2)}) %all-to-all-start) | async-done | bytes 655392 | tf_op jit(solution)/shard_map/all_to_all | solution.py:254
  34.9 0.0 copy-done
  34.9 0.0 copy-done.2
  34.9 0.0 copy-start.1
  34.9 1.0 %copy-done.1 = bf16[2048,128]{1,0:T(8,128)(2,1)S(1)} copy-done((bf16[2048,128]{1,0:T(8,128)(2,1)S(1)}, bf16[2048,128]{1,0:T(8,128)(2,1)}, u32[]{:S(2)}) %copy-start.1) | copy-done | bytes 524312
  35.9 4.1 %attend.3 = (f32[2048,256]{1,0:T(8,128)S(1)}, f32[2048,128]{1,0:T(8,128)S(1)}) custom-call(s32[8]{0:T(128)S(1)} %copy-done.2, bf16[128,2560]{1,0:T(8,128)(2,1)S(1)} %bitcast.4, bf16[2048,128]{1,0:T(8,128)(2,1)S(1)} %copy-done, bf16[2048,128]{1,0:T(8,128)(2,1)S(1)} %copy-done.1), custom_call_target="tpu_custom_call" | custom-call | tf_op jit(solution)/shard_map/attend/pallas_call | solution.py:203
  40.1 6.8 %attend.4 = (f32[2048,256]{1,0:T(8,128)S(1)}, f32[2048,128]{1,0:T(8,128)S(1)}) custom-call(s32[8]{0:T(128)S(1)} %copy-done.2, bf16[128,2560]{1,0:T(8,128)(2,1)S(1)} %bitcast.5, bf16[2048,128]{1,0:T(8,128)(2,1)S(1)} %collective-permute-done.refs_0_, bf16[2048,128]{1,0:T(8,128)(2,1)S(1)} %collective-permute-done.2.refs_1_, ...), custom_call_target="tpu_custom_call" | custom-call | tf_op jit(solution)/shard_map/attend/pallas_call | solution.py:203
  46.8 0.0 collective-permute-done.4.refs_0_
  46.9 0.0 collective-permute-done.5.refs_1_
  46.9 4.4 %attend.5 = bf16[128,2176]{1,0:T(8,128)(2,1)S(1)} custom-call(s32[8]{0:T(128)S(1)} %copy-done.2, bf16[128,2560]{1,0:T(8,128)(2,1)S(1)} %bitcast.6, bf16[2048,128]{1,0:T(8,128)(2,1)} %collective-permute-done.4.refs_0_, bf16[2048,128]{1,0:T(8,128)(2,1)} %collective-permute-done.5.refs_1_, f32[2048,256]{1,0:T(8,128)S(1)} %get-tuple-element.31.refs_2_, ...), custom_call_target="tpu_custom_call" | custom-call | tf_op jit(solution)/shard_map/attend/pallas_call | solution.py:203
  51.3 14.7 %all_to_all.10 = bf16[16,8,2176]{2,1,0:T(8,128)(2,1)S(1)} all-to-all(bf16[16,8,2176]{2,1,0:T(8,128)(2,1)S(1)} %bitcast.8), channel_id=1, replica_groups=mesh['section'=8,'kv'=16] {'kv'}, dimensions={0} | all-to-all | bytes 1114112 | tf_op jit(solution)/shard_map/all_to_all | solution.py:270
  65.9 0.5 merge.1
  66.4 0.0 collective-permute-start.6
  66.4 5.6 %collective-permute-done.6 = bf16[8,8192]{1,0:T(8,128)(2,1)S(1)} collective-permute-done((bf16[8,8192]{1,0:T(8,128)(2,1)S(1)}, bf16[8,8192]{1,0:T(8,128)(2,1)S(1)}, u32[]{:S(2)}, u32[]{:S(2)}) %collective-permute-start.6) | collective-permute-done | bytes 131104 | tf_op jit(solution)/shard_map/ppermute | solution.py:272
  72.0 0.7 copy.8
Async XLA Ops:
  4.1 14.2 %collective-permute-start = (bf16[2048,128]{1,0:T(8,128)(2,1)}, bf16[2048,128]{1,0:T(8,128)(2,1)S(1)}, u32[]{:S(2)}, u32[]{:S(2)}) collective-permute-start(bf16[2048,128]{1,0:T(8,128)(2,1)} %get-tuple-element.20), channel_id=1, source_target_pairs={{0,1},{1,0},{2,3},{3,2},{4,5},{5,4},{6,7},{7,6},{8,9},{9,8},{10,11... | collective-permute-start | bytes 1572872 | tf_op jit(solution)/shard_map/ppermute | solution.py:261
  6.2 15.7 %collective-permute-start.1 = (bf16[2048,128]{1,0:T(8,128)(2,1)}, bf16[2048,128]{1,0:T(8,128)(2,1)S(1)}, u32[]{:S(2)}, u32[]{:S(2)}) collective-permute-start(bf16[2048,128]{1,0:T(8,128)(2,1)} %get-tuple-element.21), channel_id=1, source_target_pairs={{0,3},{1,2},{2,1},{3,0},{4,7},{5,6},{6,5},{7,4},{8,11},{9,10},{10,... | collective-permute-start | bytes 1572872 | tf_op jit(solution)/shard_map/ppermute | solution.py:261
  8.7 15.1 %collective-permute-start.2 = (bf16[2048,128]{1,0:T(8,128)(2,1)}, bf16[2048,128]{1,0:T(8,128)(2,1)S(1)}, u32[]{:S(2)}, u32[]{:S(2)}) collective-permute-start(bf16[2048,128]{1,0:T(8,128)(2,1)} %get-tuple-element.22), channel_id=1, source_target_pairs={{0,4},{1,5},{2,6},{3,7},{4,0},{5,1},{6,2},{7,3},{8,12},{9,13},{10,... | collective-permute-start | bytes 1572872 | tf_op jit(solution)/shard_map/ppermute | solution.py:261
  10.3 24.6 %copy-start = (bf16[2048,128]{1,0:T(8,128)(2,1)S(1)}, bf16[2048,128]{1,0:T(8,128)(2,1)}, u32[]{:S(2)}) copy-start(bf16[2048,128]{1,0:T(8,128)(2,1)} %get-tuple-element.27.refs_0_) | copy-start | bytes 1572868
  10.3 24.6 %copy-start.2 = (s32[8]{0:T(128)S(1)}, s32[8]{0:T(128)}, u32[]{:S(2)}) copy-start(s32[8]{0:T(128)} %lengths_ref.5) | copy-start | bytes 100
  10.3 18.2 %collective-permute-start.3 = (bf16[2048,128]{1,0:T(8,128)(2,1)}, bf16[2048,128]{1,0:T(8,128)(2,1)S(1)}, u32[]{:S(2)}, u32[]{:S(2)}) collective-permute-start(bf16[2048,128]{1,0:T(8,128)(2,1)} %get-tuple-element.23), channel_id=1, source_target_pairs={{0,12},{1,13},{2,14},{3,15},{4,8},{5,9},{6,10},{7,11},{8,4},{9,5},... | collective-permute-start | bytes 1572872 | tf_op jit(solution)/shard_map/ppermute | solution.py:261
  14.3 20.6 %all-to-all-start = ((bf16[16,8,2560]{2,1,0:T(8,128)(2,1)}), bf16[16,8,2560]{2,1,0:T(8,128)(2,1)S(1)}, u32[]{:S(2)}, u32[]{:S(2)}) async-start(bf16[16,8,2560]{2,1,0:T(8,128)(2,1)} %bitcast.9), calls=%async_computation | async-start | bytes 1310720 | tf_op jit(solution)/shard_map/all_to_all | solution.py:254
  28.6 18.3 %collective-permute-start.4 = (bf16[2048,128]{1,0:T(8,128)(2,1)}, bf16[2048,128]{1,0:T(8,128)(2,1)}, u32[]{:S(2)}, u32[]{:S(2)}) collective-permute-start(bf16[2048,128]{1,0:T(8,128)(2,1)} %get-tuple-element.24), channel_id=1, source_target_pairs={{0,5},{1,4},{2,7},{3,6},{4,1},{5,0},{6,3},{7,2},{8,13},{9,12},{10,... | collective-permute-start | bytes 1572872 | tf_op jit(solution)/shard_map/ppermute | solution.py:261
  29.3 17.5 %collective-permute-start.5 = (bf16[2048,128]{1,0:T(8,128)(2,1)}, bf16[2048,128]{1,0:T(8,128)(2,1)}, u32[]{:S(2)}, u32[]{:S(2)}) collective-permute-start(bf16[2048,128]{1,0:T(8,128)(2,1)} %get-tuple-element.26), channel_id=1, source_target_pairs={{0,15},{1,14},{2,13},{3,12},{4,11},{5,10},{6,9},{7,8},{8,7},{9,6},... | collective-permute-start | bytes 1572872 | tf_op jit(solution)/shard_map/ppermute | solution.py:261
  34.9 1.0 %copy-start.1 = (bf16[2048,128]{1,0:T(8,128)(2,1)S(1)}, bf16[2048,128]{1,0:T(8,128)(2,1)}, u32[]{:S(2)}) copy-start(bf16[2048,128]{1,0:T(8,128)(2,1)} %get-tuple-element.28.refs_1_) | copy-start | bytes 1572868
  66.4 5.6 %collective-permute-start.6 = (bf16[8,8192]{1,0:T(8,128)(2,1)S(1)}, bf16[8,8192]{1,0:T(8,128)(2,1)S(1)}, u32[]{:S(2)}, u32[]{:S(2)}) collective-permute-start(bf16[8,8192]{1,0:T(8,128)(2,1)S(1)} %merge.1), channel_id=1, source_target_pairs={{0,16},{16,32},{32,48},{48,64},{64,80},{80,96},{96,112},{112,0},{1... | collective-permute-start | bytes 393224 | tf_op jit(solution)/shard_map/ppermute | solution.py:272

commit v4 on v3

--- a/solution.py
+++ b/solution.py
@@ -21,7 +21,7 @@
 LOG2E = 1.4426950408889634
 SENT = 2 * WIDE + 4 * DH
 LEVELS = 2 * GROUP
-STAGES = (((0, 0), (1, 0)), ((0, 1), (0, 2), (1, 1), (1, 2)), ((0, 3), (1, 3)))
+STAGES = (((0, 0), (0, 1), (0, 2), (1, 0), (1, 1), (1, 2)), ((0, 3), (1, 3)))
 MIB = 1024 * 1024
 CUTS = 4
 
@@ -59,7 +59,7 @@
     return pl.pallas_call(
         spread,
         out_shape=jax.ShapeDtypeStruct((SIDE * SIDE * rows, SENT), jnp.bfloat16),
-        compiler_params=pltpu.CompilerParams(vmem_limit_bytes=60 * MIB),
+        compiler_params=pltpu.CompilerParams(vmem_limit_bytes=16 * MIB),
         cost_estimate=pl.CostEstimate(flops=100_000_000_000, bytes_accessed=0, transcendentals=0),
         name="spread",
     )(queries, new_keys, new_values)
@@ -138,7 +138,8 @@
             y, z = (lax.rem(jnp.bitwise_xor(at + line, bit) - line + SIDE, SIDE) for at, bit in zip(across, flips))
             source = y * SIDE + z
             mine.append((ref[:keys], ref[keys:], places < length - source * keys))
-        sides.append([(k, jnp.concatenate([v, jnp.ones(v.shape, jnp.bfloat16)], axis=1), ok) for k, v, ok in mine])
+        k, v = (jnp.concatenate([block[i] for block in mine], axis=0) for i in range(2))
+        sides.append([(k, jnp.concatenate([v, jnp.ones(v.shape, jnp.bfloat16)], axis=1), [(b[0].shape[0], b[2]) for b in mine])])
     units = [(line, g, n) for line in range(2) for g in range(0, GROUP, AT_ONCE) for n in range(len(sides[line]))]
 
     def score(unit):
@@ -155,8 +156,12 @@
     for u, (line, g, n) in enumerate(units):
         following = score(units[u + 1]) if u + 1 < len(units) else None
         at = pl.ds((line * GROUP + g) * rows, tall)
-        _, v, ok = sides[line][n]
-        s = jnp.where(ok, s, NEG)
+        _, v, masks = sides[line][n]
+        pieces, start = [], 0
+        for width, ok in masks:
+            pieces.append(jnp.where(ok, s[:, start : start + width], NEG))
+            start += width
+        s = jnp.concatenate(pieces, axis=1)
         top = jnp.broadcast_to(jnp.max(s, axis=1, keepdims=True) * scale, (tall, DH))
         if n == 0:
             old = None if first else refs[1][at]
@@ -205,7 +210,7 @@
         in_specs=[pl.BlockSpec(memory_space=pltpu.SMEM)] + [whole] * (1 + count),
         out_specs=[whole] * len(shapes),
         out_shape=shapes,
-        compiler_params=pltpu.CompilerParams(vmem_limit_bytes=28 * MIB),
+        compiler_params=pltpu.CompilerParams(vmem_limit_bytes=44 * MIB),
         cost_estimate=pl.CostEstimate(flops=0, bytes_accessed=0, transcendentals=0),
         name="attend",
     )(lengths, q, *blocks, *state)

time: 73 us -> 71 us (0.973)
  Pallas kernels: 21.7 us -> 19.8 us
  local copies, waits for them, and re-layouts: 1.71 us -> 0.68 us
  waiting for transfers between devices: 18.7 us -> 19.6 us
    unnamed x7 -> x13, local copies, waits for them, and re-layouts: 1.71 us -> 0.68 us
    pallas_call x3 -> x2, Pallas kernels: 15.3 us -> 14.4 us  [attend_call(): pl.pallas_call(functools.partial(attend, moves, not state, last), in_spec...]
    pallas_call x1, Pallas kernels: 1.81 us -> 0.89 us  [spread_call(): pl.pallas_call(spread, out_shape=jax.ShapeDtypeStruct((SIDE * SIDE * rows...]
    ppermute x6, waiting for transfers between devices: 10.7 us -> 11.6 us  [travel(): lax.ppermute(block, 'kv', [(s, partner(s, *move)) for s in range(parts)])]
  transfers between devices with their start and end apart: 8 -> 8, of which waited for: 6 -> 6; matrix products, arithmetic and copies ran while one was open for 0% -> 0% of each run, Pallas kernels for 18% -> 15%
where the time goes in v4:
time: 71 us; the launch traced here: 70.7 us
  Pallas kernels  19.8 us (28%)
  waiting for transfers between devices  19.6 us (28%)
  starting transfers between devices  15.8 us (22%)
  blocking collectives  14.7 us (21%)
    all_to_all x1, blocking collectives, on_device(): lax.all_to_all(state[0].reshape(parts, rows, -1), 'kv', 0, 0, tiled=True)  14.7 us
    pallas_call x2, Pallas kernels, attend_call(): pl.pallas_call(functools.partial(attend, moves, not state, last), in_spec...  14.4 us
    ppermute x6, starting transfers between devices, travel(): lax.ppermute(block, 'kv', [(s, partner(s, *move)) for s in range(parts)])  12.2 us
    ppermute x6, waiting for transfers between devices, travel(): lax.ppermute(block, 'kv', [(s, partner(s, *move)) for s in range(parts)])  11.6 us
    ppermute x1, waiting for transfers between devices, on_device(): lax.ppermute(merged, 'section', [(s, (s + 1) % sections) for s in range(s...  5.59 us
    pallas_call x1, Pallas kernels, pack_call(): pl.pallas_call(functools.partial(pack, moves), in_specs=[pl.BlockSpec(mem...  4.13 us
    all_to_all x1, starting transfers between devices, on_device(): lax.all_to_all(sent.reshape(parts, rows, SENT), 'kv', 0, 0, tiled=True)  3.59 us
    all_to_all x1, waiting for transfers between devices, on_device(): lax.all_to_all(sent.reshape(parts, rows, SENT), 'kv', 0, 0, tiled=True)  2.43 us
  transfers between devices with their start and end apart: 8, of which 6 were waited for; matrix products, arithmetic and copies ran while one was open for 0% of the time, Pallas kernels for 15%

profile of v4, /device:TPU:0, one launch (start us, length us, event | category | flops | bytes accessed | tf_op | source)
XLA Modules:
  0.0 70.7 jit_solution(6576975187045754399)
XLA Ops:
  0.0 0.0 copy-start.5
  0.0 0.0 copy-start.4
  0.0 0.0 copy-start.3
  0.0 4.1 %pack.1 = (bf16[2048,128]{1,0:T(8,128)(2,1)}, bf16[2048,128]{1,0:T(8,128)(2,1)}, bf16[2048,128]{1,0:T(8,128)(2,1)}, bf16[2048,128]{1,0:T(8,128)(2,1)}, bf16[2048...) custom-call(bf16[1024,1024]{1,0:T(8,128)(2,1)} %k_ref.1, ...), custom_call_target="tpu_custom_call" | custom-call | tf_op jit(solution)/shard_map/pack/pallas_call | solution.py:97
  4.1 2.1 %collective-permute-start = (bf16[2048,128]{1,0:T(8,128)(2,1)}, bf16[2048,128]{1,0:T(8,128)(2,1)S(1)}, u32[]{:S(2)}, u32[]{:S(2)}) collective-permute-start(bf16[2048,128]{1,0:T(8,128)(2,1)} %get-tuple-element.18), channel_id=1, source_target_pairs={{0,1},{1,0},{2,3},{3,2},{4,5},{5,4},{6,7},{7,6},{8,9},{9,8},{10,11... | collective-permute-start | bytes 1572872 | tf_op jit(solution)/shard_map/ppermute | solution.py:266
  6.2 2.5 %collective-permute-start.1 = (bf16[2048,128]{1,0:T(8,128)(2,1)}, bf16[2048,128]{1,0:T(8,128)(2,1)S(1)}, u32[]{:S(2)}, u32[]{:S(2)}) collective-permute-start(bf16[2048,128]{1,0:T(8,128)(2,1)} %get-tuple-element.19), channel_id=1, source_target_pairs={{0,3},{1,2},{2,1},{3,0},{4,7},{5,6},{6,5},{7,4},{8,11},{9,10},{10,... | collective-permute-start | bytes 1572872 | tf_op jit(solution)/shard_map/ppermute | solution.py:266
  8.8 1.6 %collective-permute-start.2 = (bf16[2048,128]{1,0:T(8,128)(2,1)}, bf16[2048,128]{1,0:T(8,128)(2,1)S(1)}, u32[]{:S(2)}, u32[]{:S(2)}) collective-permute-start(bf16[2048,128]{1,0:T(8,128)(2,1)} %get-tuple-element.20), channel_id=1, source_target_pairs={{0,4},{1,5},{2,6},{3,7},{4,0},{5,1},{6,2},{7,3},{8,12},{9,13},{10,... | collective-permute-start | bytes 1572872 | tf_op jit(solution)/shard_map/ppermute | solution.py:266
  10.3 0.0 copy-start
  10.3 0.0 copy-start.1
  10.3 0.0 copy-start.2
  10.3 2.2 %collective-permute-start.3 = (bf16[2048,128]{1,0:T(8,128)(2,1)}, bf16[2048,128]{1,0:T(8,128)(2,1)}, u32[]{:S(2)}, u32[]{:S(2)}) collective-permute-start(bf16[2048,128]{1,0:T(8,128)(2,1)} %get-tuple-element.21), channel_id=1, source_target_pairs={{0,12},{1,13},{2,14},{3,15},{4,8},{5,9},{6,10},{7,11},{8,4},{9,5},... | collective-permute-start | bytes 1572872 | tf_op jit(solution)/shard_map/ppermute | solution.py:266
  12.5 0.0 copy-done.5
  12.5 0.0 copy-done.4
  12.5 0.0 copy-done.3
  12.5 0.9 %spread.1 = bf16[128,2560]{1,0:T(8,128)(2,1)} custom-call(bf16[8,8192]{1,0:T(8,128)(2,1)S(1)} %copy-done.3, bf16[8,1024]{1,0:T(8,128)(2,1)S(1)} %copy-done.4, bf16[8,1024]{1,0:T(8,128)(2,1)S(1)} %copy-done.5), custom_call_target="tpu_custom_call" | custom-call | flops 99999997952 | tf_op jit(solution)/shard_map/spread/pallas_call | solution.py:59
  13.4 3.6 %all-to-all-start = ((bf16[16,8,2560]{2,1,0:T(8,128)(2,1)}), bf16[16,8,2560]{2,1,0:T(8,128)(2,1)S(1)}, u32[]{:S(2)}, u32[]{:S(2)}) async-start(bf16[16,8,2560]{2,1,0:T(8,128)(2,1)} %bitcast), calls=%async_computation | async-start | bytes 1310720 | tf_op jit(solution)/shard_map/all_to_all | solution.py:259
  17.0 1.6 %collective-permute-done.refs_1_ = bf16[2048,128]{1,0:T(8,128)(2,1)S(1)} collective-permute-done((bf16[2048,128]{1,0:T(8,128)(2,1)}, bf16[2048,128]{1,0:T(8,128)(2,1)S(1)}, u32[]{:S(2)}, u32[]{:S(2)}) %collective-permute-start) | collective-permute-done | bytes 524320 | tf_op jit(solution)/shard_map/ppermute | solution.py:266
  18.6 3.3 %collective-permute-done.1.refs_4_ = bf16[2048,128]{1,0:T(8,128)(2,1)S(1)} collective-permute-done((bf16[2048,128]{1,0:T(8,128)(2,1)}, bf16[2048,128]{1,0:T(8,128)(2,1)S(1)}, u32[]{:S(2)}, u32[]{:S(2)}) %collective-permute-start.1) | collective-permute-done | bytes 524320 | tf_op jit(solution)/shard_map/ppermute | solution.py:266
  21.9 1.9 %collective-permute-done.2.refs_2_ = bf16[2048,128]{1,0:T(8,128)(2,1)S(1)} collective-permute-done((bf16[2048,128]{1,0:T(8,128)(2,1)}, bf16[2048,128]{1,0:T(8,128)(2,1)S(1)}, u32[]{:S(2)}, u32[]{:S(2)}) %collective-permute-start.2) | collective-permute-done | bytes 524320 | tf_op jit(solution)/shard_map/ppermute | solution.py:266
  23.8 4.8 %collective-permute-done.3.refs_5_ = bf16[2048,128]{1,0:T(8,128)(2,1)} collective-permute-done((bf16[2048,128]{1,0:T(8,128)(2,1)}, bf16[2048,128]{1,0:T(8,128)(2,1)}, u32[]{:S(2)}, u32[]{:S(2)}) %collective-permute-start.3) | collective-permute-done | bytes 524320 | tf_op jit(solution)/shard_map/ppermute | solution.py:266
  28.6 0.9 %collective-permute-start.4 = (bf16[2048,128]{1,0:T(8,128)(2,1)}, bf16[2048,128]{1,0:T(8,128)(2,1)}, u32[]{:S(2)}, u32[]{:S(2)}) collective-permute-start(bf16[2048,128]{1,0:T(8,128)(2,1)} %get-tuple-element.22), channel_id=1, source_target_pairs={{0,5},{1,4},{2,7},{3,6},{4,1},{5,0},{6,3},{7,2},{8,13},{9,12},{10,... | collective-permute-start | bytes 1572872 | tf_op jit(solution)/shard_map/ppermute | solution.py:266
  29.4 3.0 %collective-permute-start.5 = (bf16[2048,128]{1,0:T(8,128)(2,1)}, bf16[2048,128]{1,0:T(8,128)(2,1)}, u32[]{:S(2)}, u32[]{:S(2)}) collective-permute-start(bf16[2048,128]{1,0:T(8,128)(2,1)} %get-tuple-element.24), channel_id=1, source_target_pairs={{0,15},{1,14},{2,13},{3,12},{4,11},{5,10},{6,9},{7,8},{8,7},{9,6},... | collective-permute-start | bytes 1572872 | tf_op jit(solution)/shard_map/ppermute | solution.py:266
  32.5 2.4 %all-to-all-done = bf16[16,8,2560]{2,1,0:T(8,128)(2,1)S(1)} async-done(((bf16[16,8,2560]{2,1,0:T(8,128)(2,1)}), bf16[16,8,2560]{2,1,0:T(8,128)(2,1)S(1)}, u32[]{:S(2)}, u32[]{:S(2)}) %all-to-all-start) | async-done | bytes 655392 | tf_op jit(solution)/shard_map/all_to_all | solution.py:259
  34.9 0.0 copy-done
  34.9 0.0 copy-done.1
  34.9 0.0 copy-done.2
  34.9 9.8 %attend.2 = (f32[2048,256]{1,0:T(8,128)S(1)}, f32[2048,128]{1,0:T(8,128)S(1)}) custom-call(s32[8]{0:T(128)S(1)} %copy-done.2, bf16[128,2560]{1,0:T(8,128)(2,1)S(1)} %bitcast.4, bf16[2048,128]{1,0:T(8,128)(2,1)S(1)} %copy-done, bf16[2048,128]{1,0:T(8,128)(2,1)S(1)} %collective-permute-done.refs_1_, bf16[2048,128]{1,0:T(8,128)(2,1)S(1)} %collective-permute-done.2.refs_2_, ...), custom_call_target="tpu_custom_call" | custom-call | tf_op jit(solution)/shard_map/attend/pallas_call | solution.py:208
  44.8 0.0 collective-permute-done.4.refs_0_
  44.8 0.0 collective-permute-done.5.refs_1_
  44.8 4.5 %attend.3 = bf16[128,2176]{1,0:T(8,128)(2,1)S(1)} custom-call(s32[8]{0:T(128)S(1)} %copy-done.2, bf16[128,2560]{1,0:T(8,128)(2,1)S(1)} %bitcast.5, bf16[2048,128]{1,0:T(8,128)(2,1)} %collective-permute-done.4.refs_0_, bf16[2048,128]{1,0:T(8,128)(2,1)} %collective-permute-done.5.refs_1_, f32[2048,256]{1,0:T(8,128)S(1)} %get-tuple-element.27.refs_2_, ...), custom_call_target="tpu_custom_call" | custom-call | tf_op jit(solution)/shard_map/attend/pallas_call | solution.py:208
  49.3 14.7 %all_to_all.10 = bf16[16,8,2176]{2,1,0:T(8,128)(2,1)S(1)} all-to-all(bf16[16,8,2176]{2,1,0:T(8,128)(2,1)S(1)} %bitcast.7), channel_id=1, replica_groups=mesh['section'=8,'kv'=16] {'kv'}, dimensions={0} | all-to-all | bytes 1114112 | tf_op jit(solution)/shard_map/all_to_all | solution.py:275
  64.0 0.5 merge.1
  64.4 0.0 collective-permute-start.6
  64.5 5.6 %collective-permute-done.6 = bf16[8,8192]{1,0:T(8,128)(2,1)S(1)} collective-permute-done((bf16[8,8192]{1,0:T(8,128)(2,1)S(1)}, bf16[8,8192]{1,0:T(8,128)(2,1)S(1)}, u32[]{:S(2)}, u32[]{:S(2)}) %collective-permute-start.6) | collective-permute-done | bytes 131104 | tf_op jit(solution)/shard_map/ppermute | solution.py:277
  70.0 0.7 copy.8
Async XLA Ops:
  0.0 12.5 %copy-start.5 = (bf16[8,1024]{1,0:T(8,128)(2,1)S(1)}, bf16[8,1024]{1,0:T(8,128)(2,1)}, u32[]{:S(2)}) copy-start(bf16[8,1024]{1,0:T(8,128)(2,1)} %nv_ref.1) | copy-start | bytes 49156
  0.0 12.5 %copy-start.4 = (bf16[8,1024]{1,0:T(8,128)(2,1)S(1)}, bf16[8,1024]{1,0:T(8,128)(2,1)}, u32[]{:S(2)}) copy-start(bf16[8,1024]{1,0:T(8,128)(2,1)} %nk_ref.1) | copy-start | bytes 49156
  0.0 12.5 %copy-start.3 = (bf16[8,8192]{1,0:T(8,128)(2,1)S(1)}, bf16[8,8192]{1,0:T(8,128)(2,1)}, u32[]{:S(2)}) copy-start(bf16[8,8192]{1,0:T(8,128)(2,1)} %q_ref.1) | copy-start | bytes 393220
  4.1 14.5 %collective-permute-start = (bf16[2048,128]{1,0:T(8,128)(2,1)}, bf16[2048,128]{1,0:T(8,128)(2,1)S(1)}, u32[]{:S(2)}, u32[]{:S(2)}) collective-permute-start(bf16[2048,128]{1,0:T(8,128)(2,1)} %get-tuple-element.18), channel_id=1, source_target_pairs={{0,1},{1,0},{2,3},{3,2},{4,5},{5,4},{6,7},{7,6},{8,9},{9,8},{10,11... | collective-permute-start | bytes 1572872 | tf_op jit(solution)/shard_map/ppermute | solution.py:266
  6.2 15.7 %collective-permute-start.1 = (bf16[2048,128]{1,0:T(8,128)(2,1)}, bf16[2048,128]{1,0:T(8,128)(2,1)S(1)}, u32[]{:S(2)}, u32[]{:S(2)}) collective-permute-start(bf16[2048,128]{1,0:T(8,128)(2,1)} %get-tuple-element.19), channel_id=1, source_target_pairs={{0,3},{1,2},{2,1},{3,0},{4,7},{5,6},{6,5},{7,4},{8,11},{9,10},{10,... | collective-permute-start | bytes 1572872 | tf_op jit(solution)/shard_map/ppermute | solution.py:266
  8.8 15.1 %collective-permute-start.2 = (bf16[2048,128]{1,0:T(8,128)(2,1)}, bf16[2048,128]{1,0:T(8,128)(2,1)S(1)}, u32[]{:S(2)}, u32[]{:S(2)}) collective-permute-start(bf16[2048,128]{1,0:T(8,128)(2,1)} %get-tuple-element.20), channel_id=1, source_target_pairs={{0,4},{1,5},{2,6},{3,7},{4,0},{5,1},{6,2},{7,3},{8,12},{9,13},{10,... | collective-permute-start | bytes 1572872 | tf_op jit(solution)/shard_map/ppermute | solution.py:266
  10.3 24.6 %copy-start = (bf16[2048,128]{1,0:T(8,128)(2,1)S(1)}, bf16[2048,128]{1,0:T(8,128)(2,1)}, u32[]{:S(2)}) copy-start(bf16[2048,128]{1,0:T(8,128)(2,1)} %get-tuple-element.25.refs_0_) | copy-start | bytes 1572868
  10.3 24.6 %copy-start.1 = (bf16[2048,128]{1,0:T(8,128)(2,1)S(1)}, bf16[2048,128]{1,0:T(8,128)(2,1)}, u32[]{:S(2)}) copy-start(bf16[2048,128]{1,0:T(8,128)(2,1)} %get-tuple-element.26.refs_3_) | copy-start | bytes 1572868
  10.3 24.6 %copy-start.2 = (s32[8]{0:T(128)S(1)}, s32[8]{0:T(128)}, u32[]{:S(2)}) copy-start(s32[8]{0:T(128)} %lengths_ref.3) | copy-start | bytes 100
  10.3 18.2 %collective-permute-start.3 = (bf16[2048,128]{1,0:T(8,128)(2,1)}, bf16[2048,128]{1,0:T(8,128)(2,1)}, u32[]{:S(2)}, u32[]{:S(2)}) collective-permute-start(bf16[2048,128]{1,0:T(8,128)(2,1)} %get-tuple-element.21), channel_id=1, source_target_pairs={{0,12},{1,13},{2,14},{3,15},{4,8},{5,9},{6,10},{7,11},{8,4},{9,5},... | collective-permute-start | bytes 1572872 | tf_op jit(solution)/shard_map/ppermute | solution.py:266
  13.4 21.5 %all-to-all-start = ((bf16[16,8,2560]{2,1,0:T(8,128)(2,1)}), bf16[16,8,2560]{2,1,0:T(8,128)(2,1)S(1)}, u32[]{:S(2)}, u32[]{:S(2)}) async-start(bf16[16,8,2560]{2,1,0:T(8,128)(2,1)} %bitcast), calls=%async_computation | async-start | bytes 1310720 | tf_op jit(solution)/shard_map/all_to_all | solution.py:259
  28.6 16.2 %collective-permute-start.4 = (bf16[2048,128]{1,0:T(8,128)(2,1)}, bf16[2048,128]{1,0:T(8,128)(2,1)}, u32[]{:S(2)}, u32[]{:S(2)}) collective-permute-start(bf16[2048,128]{1,0:T(8,128)(2,1)} %get-tuple-element.22), channel_id=1, source_target_pairs={{0,5},{1,4},{2,7},{3,6},{4,1},{5,0},{6,3},{7,2},{8,13},{9,12},{10,... | collective-permute-start | bytes 1572872 | tf_op jit(solution)/shard_map/ppermute | solution.py:266
  29.4 15.3 %collective-permute-start.5 = (bf16[2048,128]{1,0:T(8,128)(2,1)}, bf16[2048,128]{1,0:T(8,128)(2,1)}, u32[]{:S(2)}, u32[]{:S(2)}) collective-permute-start(bf16[2048,128]{1,0:T(8,128)(2,1)} %get-tuple-element.24), channel_id=1, source_target_pairs={{0,15},{1,14},{2,13},{3,12},{4,11},{5,10},{6,9},{7,8},{8,7},{9,6},... | collective-permute-start | bytes 1572872 | tf_op jit(solution)/shard_map/ppermute | solution.py:266
  64.4 5.6 %collective-permute-start.6 = (bf16[8,8192]{1,0:T(8,128)(2,1)S(1)}, bf16[8,8192]{1,0:T(8,128)(2,1)S(1)}, u32[]{:S(2)}, u32[]{:S(2)}) collective-permute-start(bf16[8,8192]{1,0:T(8,128)(2,1)S(1)} %merge.1), channel_id=1, source_target_pairs={{0,16},{16,32},{32,48},{48,64},{64,80},{80,96},{96,112},{112,0},{1... | collective-permute-start | bytes 393224 | tf_op jit(solution)/shard_map/ppermute | solution.py:277

commit v5 on v4

--- a/solution.py
+++ b/solution.py
@@ -23,7 +23,7 @@
 LEVELS = 2 * GROUP
 STAGES = (((0, 0), (0, 1), (0, 2), (1, 0), (1, 1), (1, 2)), ((0, 3), (1, 3)))
 MIB = 1024 * 1024
-CUTS = 4
+CUTS = 2
 
 
 def contract(left, right, dim):

time: 71 us -> 70.4 us (level)
  no operation moved by 1% of the time
where the time goes in v5:
time: 70.4 us; the launch traced here: 70.1 us
  waiting for transfers between devices  19.6 us (28%)
  Pallas kernels  19.3 us (27%)
  starting transfers between devices  15.8 us (22%)
  blocking collectives  14.7 us (21%)
    all_to_all x1, blocking collectives, on_device(): lax.all_to_all(state[0].reshape(parts, rows, -1), 'kv', 0, 0, tiled=True)  14.7 us
    pallas_call x2, Pallas kernels, attend_call(): pl.pallas_call(functools.partial(attend, moves, not state, last), in_spec...  14.4 us
    ppermute x6, starting transfers between devices, travel(): lax.ppermute(block, 'kv', [(s, partner(s, *move)) for s in range(parts)])  12.2 us
    ppermute x6, waiting for transfers between devices, travel(): lax.ppermute(block, 'kv', [(s, partner(s, *move)) for s in range(parts)])  11.6 us
    ppermute x1, waiting for transfers between devices, on_device(): lax.ppermute(merged, 'section', [(s, (s + 1) % sections) for s in range(s...  5.59 us
    all_to_all x1, starting transfers between devices, on_device(): lax.all_to_all(sent.reshape(parts, rows, SENT), 'kv', 0, 0, tiled=True)  3.59 us
    pallas_call x1, Pallas kernels, pack_call(): pl.pallas_call(functools.partial(pack, moves), in_specs=[pl.BlockSpec(mem...  3.55 us
    all_to_all x1, waiting for transfers between devices, on_device(): lax.all_to_all(sent.reshape(parts, rows, SENT), 'kv', 0, 0, tiled=True)  2.43 us
  transfers between devices with their start and end apart: 8, of which 6 were waited for; matrix products, arithmetic and copies ran while one was open for 0% of the time, Pallas kernels for 15%

profile of v5, /device:TPU:0, one launch (start us, length us, event | category | flops | bytes accessed | tf_op | source)
XLA Modules:
  0.0 70.1 jit_solution(17960933092925630377)
XLA Ops:
  0.0 0.0 copy-start.5
  0.0 0.0 copy-start.4
  0.0 0.0 copy-start.3
  0.0 3.6 %pack.1 = (bf16[2048,128]{1,0:T(8,128)(2,1)}, bf16[2048,128]{1,0:T(8,128)(2,1)}, bf16[2048,128]{1,0:T(8,128)(2,1)}, bf16[2048,128]{1,0:T(8,128)(2,1)}, bf16[2048...) custom-call(bf16[1024,1024]{1,0:T(8,128)(2,1)} %k_ref.1, ...), custom_call_target="tpu_custom_call" | custom-call | tf_op jit(solution)/shard_map/pack/pallas_call | solution.py:97
  3.6 2.1 %collective-permute-start = (bf16[2048,128]{1,0:T(8,128)(2,1)}, bf16[2048,128]{1,0:T(8,128)(2,1)S(1)}, u32[]{:S(2)}, u32[]{:S(2)}) collective-permute-start(bf16[2048,128]{1,0:T(8,128)(2,1)} %get-tuple-element.18), channel_id=1, source_target_pairs={{0,1},{1,0},{2,3},{3,2},{4,5},{5,4},{6,7},{7,6},{8,9},{9,8},{10,11... | collective-permute-start | bytes 1572872 | tf_op jit(solution)/shard_map/ppermute | solution.py:266
  5.7 2.5 %collective-permute-start.1 = (bf16[2048,128]{1,0:T(8,128)(2,1)}, bf16[2048,128]{1,0:T(8,128)(2,1)S(1)}, u32[]{:S(2)}, u32[]{:S(2)}) collective-permute-start(bf16[2048,128]{1,0:T(8,128)(2,1)} %get-tuple-element.19), channel_id=1, source_target_pairs={{0,3},{1,2},{2,1},{3,0},{4,7},{5,6},{6,5},{7,4},{8,11},{9,10},{10,... | collective-permute-start | bytes 1572872 | tf_op jit(solution)/shard_map/ppermute | solution.py:266
  8.2 1.6 %collective-permute-start.2 = (bf16[2048,128]{1,0:T(8,128)(2,1)}, bf16[2048,128]{1,0:T(8,128)(2,1)S(1)}, u32[]{:S(2)}, u32[]{:S(2)}) collective-permute-start(bf16[2048,128]{1,0:T(8,128)(2,1)} %get-tuple-element.20), channel_id=1, source_target_pairs={{0,4},{1,5},{2,6},{3,7},{4,0},{5,1},{6,2},{7,3},{8,12},{9,13},{10,... | collective-permute-start | bytes 1572872 | tf_op jit(solution)/shard_map/ppermute | solution.py:266
  9.8 0.0 copy-start
  9.8 0.0 copy-start.1
  9.8 0.0 copy-start.2
  9.8 2.2 %collective-permute-start.3 = (bf16[2048,128]{1,0:T(8,128)(2,1)}, bf16[2048,128]{1,0:T(8,128)(2,1)}, u32[]{:S(2)}, u32[]{:S(2)}) collective-permute-start(bf16[2048,128]{1,0:T(8,128)(2,1)} %get-tuple-element.21), channel_id=1, source_target_pairs={{0,12},{1,13},{2,14},{3,15},{4,8},{5,9},{6,10},{7,11},{8,4},{9,5},... | collective-permute-start | bytes 1572872 | tf_op jit(solution)/shard_map/ppermute | solution.py:266
  11.9 0.0 copy-done.5
  11.9 0.0 copy-done.4
  12.0 0.0 copy-done.3
  12.0 0.9 %spread.1 = bf16[128,2560]{1,0:T(8,128)(2,1)} custom-call(bf16[8,8192]{1,0:T(8,128)(2,1)S(1)} %copy-done.3, bf16[8,1024]{1,0:T(8,128)(2,1)S(1)} %copy-done.4, bf16[8,1024]{1,0:T(8,128)(2,1)S(1)} %copy-done.5), custom_call_target="tpu_custom_call" | custom-call | flops 99999997952 | tf_op jit(solution)/shard_map/spread/pallas_call | solution.py:59
  12.8 3.6 %all-to-all-start = ((bf16[16,8,2560]{2,1,0:T(8,128)(2,1)}), bf16[16,8,2560]{2,1,0:T(8,128)(2,1)S(1)}, u32[]{:S(2)}, u32[]{:S(2)}) async-start(bf16[16,8,2560]{2,1,0:T(8,128)(2,1)} %bitcast), calls=%async_computation | async-start | bytes 1310720 | tf_op jit(solution)/shard_map/all_to_all | solution.py:259
  16.4 1.6 %collective-permute-done.refs_1_ = bf16[2048,128]{1,0:T(8,128)(2,1)S(1)} collective-permute-done((bf16[2048,128]{1,0:T(8,128)(2,1)}, bf16[2048,128]{1,0:T(8,128)(2,1)S(1)}, u32[]{:S(2)}, u32[]{:S(2)}) %collective-permute-start) | collective-permute-done | bytes 524320 | tf_op jit(solution)/shard_map/ppermute | solution.py:266
  18.0 3.3 %collective-permute-done.1.refs_4_ = bf16[2048,128]{1,0:T(8,128)(2,1)S(1)} collective-permute-done((bf16[2048,128]{1,0:T(8,128)(2,1)}, bf16[2048,128]{1,0:T(8,128)(2,1)S(1)}, u32[]{:S(2)}, u32[]{:S(2)}) %collective-permute-start.1) | collective-permute-done | bytes 524320 | tf_op jit(solution)/shard_map/ppermute | solution.py:266
  21.3 1.9 %collective-permute-done.2.refs_2_ = bf16[2048,128]{1,0:T(8,128)(2,1)S(1)} collective-permute-done((bf16[2048,128]{1,0:T(8,128)(2,1)}, bf16[2048,128]{1,0:T(8,128)(2,1)S(1)}, u32[]{:S(2)}, u32[]{:S(2)}) %collective-permute-start.2) | collective-permute-done | bytes 524320 | tf_op jit(solution)/shard_map/ppermute | solution.py:266
  23.3 4.8 %collective-permute-done.3.refs_5_ = bf16[2048,128]{1,0:T(8,128)(2,1)} collective-permute-done((bf16[2048,128]{1,0:T(8,128)(2,1)}, bf16[2048,128]{1,0:T(8,128)(2,1)}, u32[]{:S(2)}, u32[]{:S(2)}) %collective-permute-start.3) | collective-permute-done | bytes 524320 | tf_op jit(solution)/shard_map/ppermute | solution.py:266
  28.0 0.9 %collective-permute-start.4 = (bf16[2048,128]{1,0:T(8,128)(2,1)}, bf16[2048,128]{1,0:T(8,128)(2,1)}, u32[]{:S(2)}, u32[]{:S(2)}) collective-permute-start(bf16[2048,128]{1,0:T(8,128)(2,1)} %get-tuple-element.22), channel_id=1, source_target_pairs={{0,5},{1,4},{2,7},{3,6},{4,1},{5,0},{6,3},{7,2},{8,13},{9,12},{10,... | collective-permute-start | bytes 1572872 | tf_op jit(solution)/shard_map/ppermute | solution.py:266
  28.9 3.0 %collective-permute-start.5 = (bf16[2048,128]{1,0:T(8,128)(2,1)}, bf16[2048,128]{1,0:T(8,128)(2,1)}, u32[]{:S(2)}, u32[]{:S(2)}) collective-permute-start(bf16[2048,128]{1,0:T(8,128)(2,1)} %get-tuple-element.24), channel_id=1, source_target_pairs={{0,15},{1,14},{2,13},{3,12},{4,11},{5,10},{6,9},{7,8},{8,7},{9,6},... | collective-permute-start | bytes 1572872 | tf_op jit(solution)/shard_map/ppermute | solution.py:266
  31.9 2.4 %all-to-all-done = bf16[16,8,2560]{2,1,0:T(8,128)(2,1)S(1)} async-done(((bf16[16,8,2560]{2,1,0:T(8,128)(2,1)}), bf16[16,8,2560]{2,1,0:T(8,128)(2,1)S(1)}, u32[]{:S(2)}, u32[]{:S(2)}) %all-to-all-start) | async-done | bytes 655392 | tf_op jit(solution)/shard_map/all_to_all | solution.py:259
  34.3 0.0 copy-done
  34.3 0.0 copy-done.1
  34.3 0.0 copy-done.2
  34.3 9.8 %attend.2 = (f32[2048,256]{1,0:T(8,128)S(1)}, f32[2048,128]{1,0:T(8,128)S(1)}) custom-call(s32[8]{0:T(128)S(1)} %copy-done.2, bf16[128,2560]{1,0:T(8,128)(2,1)S(1)} %bitcast.4, bf16[2048,128]{1,0:T(8,128)(2,1)S(1)} %copy-done, bf16[2048,128]{1,0:T(8,128)(2,1)S(1)} %collective-permute-done.refs_1_, bf16[2048,128]{1,0:T(8,128)(2,1)S(1)} %collective-permute-done.2.refs_2_, ...), custom_call_target="tpu_custom_call" | custom-call | tf_op jit(solution)/shard_map/attend/pallas_call | solution.py:208
  44.2 0.0 collective-permute-done.4.refs_0_
  44.2 0.0 collective-permute-done.5.refs_1_
  44.2 4.5 %attend.3 = bf16[128,2176]{1,0:T(8,128)(2,1)S(1)} custom-call(s32[8]{0:T(128)S(1)} %copy-done.2, bf16[128,2560]{1,0:T(8,128)(2,1)S(1)} %bitcast.5, bf16[2048,128]{1,0:T(8,128)(2,1)} %collective-permute-done.4.refs_0_, bf16[2048,128]{1,0:T(8,128)(2,1)} %collective-permute-done.5.refs_1_, f32[2048,256]{1,0:T(8,128)S(1)} %get-tuple-element.27.refs_2_, ...), custom_call_target="tpu_custom_call" | custom-call | tf_op jit(solution)/shard_map/attend/pallas_call | solution.py:208
  48.7 14.7 %all_to_all.10 = bf16[16,8,2176]{2,1,0:T(8,128)(2,1)S(1)} all-to-all(bf16[16,8,2176]{2,1,0:T(8,128)(2,1)S(1)} %bitcast.7), channel_id=1, replica_groups=mesh['section'=8,'kv'=16] {'kv'}, dimensions={0} | all-to-all | bytes 1114112 | tf_op jit(solution)/shard_map/all_to_all | solution.py:275
  63.4 0.5 merge.1
  63.8 0.0 collective-permute-start.6
  63.9 5.6 %collective-permute-done.6 = bf16[8,8192]{1,0:T(8,128)(2,1)S(1)} collective-permute-done((bf16[8,8192]{1,0:T(8,128)(2,1)S(1)}, bf16[8,8192]{1,0:T(8,128)(2,1)S(1)}, u32[]{:S(2)}, u32[]{:S(2)}) %collective-permute-start.6) | collective-permute-done | bytes 131104 | tf_op jit(solution)/shard_map/ppermute | solution.py:277
  69.5 0.7 copy.8
Async XLA Ops:
  0.0 11.9 %copy-start.5 = (bf16[8,1024]{1,0:T(8,128)(2,1)S(1)}, bf16[8,1024]{1,0:T(8,128)(2,1)}, u32[]{:S(2)}) copy-start(bf16[8,1024]{1,0:T(8,128)(2,1)} %nv_ref.1) | copy-start | bytes 49156
  0.0 11.9 %copy-start.4 = (bf16[8,1024]{1,0:T(8,128)(2,1)S(1)}, bf16[8,1024]{1,0:T(8,128)(2,1)}, u32[]{:S(2)}) copy-start(bf16[8,1024]{1,0:T(8,128)(2,1)} %nk_ref.1) | copy-start | bytes 49156
  0.0 11.9 %copy-start.3 = (bf16[8,8192]{1,0:T(8,128)(2,1)S(1)}, bf16[8,8192]{1,0:T(8,128)(2,1)}, u32[]{:S(2)}) copy-start(bf16[8,8192]{1,0:T(8,128)(2,1)} %q_ref.1) | copy-start | bytes 393220
  3.6 14.5 %collective-permute-start = (bf16[2048,128]{1,0:T(8,128)(2,1)}, bf16[2048,128]{1,0:T(8,128)(2,1)S(1)}, u32[]{:S(2)}, u32[]{:S(2)}) collective-permute-start(bf16[2048,128]{1,0:T(8,128)(2,1)} %get-tuple-element.18), channel_id=1, source_target_pairs={{0,1},{1,0},{2,3},{3,2},{4,5},{5,4},{6,7},{7,6},{8,9},{9,8},{10,11... | collective-permute-start | bytes 1572872 | tf_op jit(solution)/shard_map/ppermute | solution.py:266
  5.7 15.7 %collective-permute-start.1 = (bf16[2048,128]{1,0:T(8,128)(2,1)}, bf16[2048,128]{1,0:T(8,128)(2,1)S(1)}, u32[]{:S(2)}, u32[]{:S(2)}) collective-permute-start(bf16[2048,128]{1,0:T(8,128)(2,1)} %get-tuple-element.19), channel_id=1, source_target_pairs={{0,3},{1,2},{2,1},{3,0},{4,7},{5,6},{6,5},{7,4},{8,11},{9,10},{10,... | collective-permute-start | bytes 1572872 | tf_op jit(solution)/shard_map/ppermute | solution.py:266
  8.2 15.1 %collective-permute-start.2 = (bf16[2048,128]{1,0:T(8,128)(2,1)}, bf16[2048,128]{1,0:T(8,128)(2,1)S(1)}, u32[]{:S(2)}, u32[]{:S(2)}) collective-permute-start(bf16[2048,128]{1,0:T(8,128)(2,1)} %get-tuple-element.20), channel_id=1, source_target_pairs={{0,4},{1,5},{2,6},{3,7},{4,0},{5,1},{6,2},{7,3},{8,12},{9,13},{10,... | collective-permute-start | bytes 1572872 | tf_op jit(solution)/shard_map/ppermute | solution.py:266
  9.8 24.6 %copy-start = (bf16[2048,128]{1,0:T(8,128)(2,1)S(1)}, bf16[2048,128]{1,0:T(8,128)(2,1)}, u32[]{:S(2)}) copy-start(bf16[2048,128]{1,0:T(8,128)(2,1)} %get-tuple-element.25.refs_0_) | copy-start | bytes 1572868
  9.8 24.6 %copy-start.1 = (bf16[2048,128]{1,0:T(8,128)(2,1)S(1)}, bf16[2048,128]{1,0:T(8,128)(2,1)}, u32[]{:S(2)}) copy-start(bf16[2048,128]{1,0:T(8,128)(2,1)} %get-tuple-element.26.refs_3_) | copy-start | bytes 1572868
  9.8 24.6 %copy-start.2 = (s32[8]{0:T(128)S(1)}, s32[8]{0:T(128)}, u32[]{:S(2)}) copy-start(s32[8]{0:T(128)} %lengths_ref.3) | copy-start | bytes 100
  9.8 18.2 %collective-permute-start.3 = (bf16[2048,128]{1,0:T(8,128)(2,1)}, bf16[2048,128]{1,0:T(8,128)(2,1)}, u32[]{:S(2)}, u32[]{:S(2)}) collective-permute-start(bf16[2048,128]{1,0:T(8,128)(2,1)} %get-tuple-element.21), channel_id=1, source_target_pairs={{0,12},{1,13},{2,14},{3,15},{4,8},{5,9},{6,10},{7,11},{8,4},{9,5},... | collective-permute-start | bytes 1572872 | tf_op jit(solution)/shard_map/ppermute | solution.py:266
  12.8 21.5 %all-to-all-start = ((bf16[16,8,2560]{2,1,0:T(8,128)(2,1)}), bf16[16,8,2560]{2,1,0:T(8,128)(2,1)S(1)}, u32[]{:S(2)}, u32[]{:S(2)}) async-start(bf16[16,8,2560]{2,1,0:T(8,128)(2,1)} %bitcast), calls=%async_computation | async-start | bytes 1310720 | tf_op jit(solution)/shard_map/all_to_all | solution.py:259
  28.0 16.2 %collective-permute-start.4 = (bf16[2048,128]{1,0:T(8,128)(2,1)}, bf16[2048,128]{1,0:T(8,128)(2,1)}, u32[]{:S(2)}, u32[]{:S(2)}) collective-permute-start(bf16[2048,128]{1,0:T(8,128)(2,1)} %get-tuple-element.22), channel_id=1, source_target_pairs={{0,5},{1,4},{2,7},{3,6},{4,1},{5,0},{6,3},{7,2},{8,13},{9,12},{10,... | collective-permute-start | bytes 1572872 | tf_op jit(solution)/shard_map/ppermute | solution.py:266
  28.9 15.3 %collective-permute-start.5 = (bf16[2048,128]{1,0:T(8,128)(2,1)}, bf16[2048,128]{1,0:T(8,128)(2,1)}, u32[]{:S(2)}, u32[]{:S(2)}) collective-permute-start(bf16[2048,128]{1,0:T(8,128)(2,1)} %get-tuple-element.24), channel_id=1, source_target_pairs={{0,15},{1,14},{2,13},{3,12},{4,11},{5,10},{6,9},{7,8},{8,7},{9,6},... | collective-permute-start | bytes 1572872 | tf_op jit(solution)/shard_map/ppermute | solution.py:266
  63.8 5.6 %collective-permute-start.6 = (bf16[8,8192]{1,0:T(8,128)(2,1)S(1)}, bf16[8,8192]{1,0:T(8,128)(2,1)S(1)}, u32[]{:S(2)}, u32[]{:S(2)}) collective-permute-start(bf16[8,8192]{1,0:T(8,128)(2,1)S(1)} %merge.1), channel_id=1, source_target_pairs={{0,16},{16,32},{32,48},{48,64},{64,80},{80,96},{96,112},{112,0},{1... | collective-permute-start | bytes 393224 | tf_op jit(solution)/shard_map/ppermute | solution.py:277
